TPU v7x, 32 devices: a whole 2x2x4 slice. The times are simulated.
32 devices in a mesh: face: 2 (over x), tile: 16 (over z, y, core).
Axes of the slice: x: 2, y: 2, z: 4, core: 2. Of those that a mesh axis runs over, the one named last changes fastest.
Arguments:
- maps: bfloat16 [4, 4, 32, 2048], P(None, None, 'face', 'tile'), may hold values from -8 to 8
- params: float32 [4, 2], replicated, may hold values from 0 to 1
- labels: int32 [4], replicated, may hold values 0 or 1
- edge_flip: int32 [2, 16], replicated, may hold values from 0 to 1
- fine_weight: float32 [3, 4, 16], replicated, may hold values from -1.75 to 1.75
- coarse_weight: float32 [3, 16, 32], replicated, may hold values from -0.875 to 0.875
- feature_weight: float32 [32, 128], replicated, may hold values from -2 to 2
- param_weight: float32 [2, 128], replicated, may hold values from -4 to 4
- out_weight: float32 [128], replicated, may hold values from -1 to 1
Outputs:
- logits: float32 [4], replicated
- saliency: float32 [4, 4, 32, 2048], P(None, None, 'face', 'tile')
- grad_fine: float32 [3, 4, 16], replicated
- grad_coarse: float32 [3, 16, 32], replicated
All inputs are finite; a program needn't handle non-finite values.
Results may differ from a plain program's by a relative error of at most 0.0003.
Values sent between devices are 32-bit elements; how exact they have to be, the bound alone decides.
A program may use at most 64 MiB of HBM per device.

v0:
```python
import jax
import jax.numpy as jnp
from jax import lax
from jax.sharding import PartitionSpec as P

exact = lax.Precision.HIGHEST


def with_halo(block, sides, width):
    for axis, dim in sides:
        count = lax.axis_size(axis)
        forward = [(i, i + 1) for i in range(count - 1)]
        forward.append((count - 1, 0))
        backward = [(target, source) for source, target in forward]
        low = lax.ppermute(
            lax.slice_in_dim(block, block.shape[dim] - width, None, axis=dim), axis, forward
        )
        high = lax.ppermute(lax.slice_in_dim(block, 0, width, axis=dim), axis, backward)
        block = jnp.concatenate([low, block, high], axis=dim)
    return block


def turn_blocks(edge_row, width):
    lead = edge_row.shape[:-1]
    return edge_row.reshape(lead + (-1, width))[..., ::-1].reshape(edge_row.shape)


def face_flags(edge_flip):
    position = lax.axis_index("face")
    faces = edge_flip.shape[0]
    return (edge_flip[position] == 1, edge_flip[(position + 1) % faces] == 1)


def tile_flags(flags):
    tiles = flags[0].shape[0]
    spot = lax.axis_index("tile") % tiles
    return (flags[0][spot], flags[1][spot])


def stencil(padded, flags, width):
    top_flag, bottom_flag = tile_flags(flags)
    left = padded[..., 1:-1, :-2]
    right = padded[..., 1:-1, 2:]
    upper = padded[..., :-2, 1:-1]
    lower = padded[..., 2:, 1:-1]
    top_row = upper[..., 0, :]
    upper = upper.at[..., 0, :].set(jnp.where(top_flag, turn_blocks(top_row, width), top_row))
    bottom_row = lower[..., -1, :]
    lower = lower.at[..., -1, :].set(
        jnp.where(bottom_flag, turn_blocks(bottom_row, width), bottom_row)
    )
    return -0.25 * (upper + lower + left + right)


def fine_apply(field, flags):
    padded = with_halo(field, (("face", 2), ("tile", 3)), 1)
    return stencil(padded, flags, field.shape[-1])


def coarse_apply(field, flags):
    padded = with_halo(field, (("face", 2), ("tile", 3)), 1)
    return stencil(padded, flags, field.shape[-1])


def coarse_terms(field, flags):
    first = coarse_apply(field, flags)
    second = 2.0 * coarse_apply(first, flags) - field
    return (first, second)


def coarse_adjoint(parts, flags):
    inner = coarse_apply(parts[2], flags)
    outer = coarse_apply(parts[1] + 2.0 * inner, flags)
    return parts[0] - parts[2] + outer


def on_device(
    maps,
    params,
    labels,
    edge_flip,
    fine_weight,
    coarse_weight,
    feature_weight,
    param_weight,
    out_weight,
):
    flags = face_flags(edge_flip)
    field0 = maps.astype(jnp.float32)
    first0 = fine_apply(field0, flags)
    second0 = 2.0 * fine_apply(first0, flags) - field0
    terms0 = jnp.stack([field0, first0, second0])
    pre0 = jnp.einsum("kio,kbirc->borc", fine_weight, terms0, precision=exact)
    act0 = jax.nn.softplus(pre0)
    nmaps, nchan, nrows, ncols = act0.shape
    field1 = act0.reshape(nmaps, nchan, nrows // 2, 2, ncols // 2, 2).mean(axis=(3, 5))
    first1, second1 = coarse_terms(field1, flags)
    terms1 = jnp.stack([field1, first1, second1])
    pre1 = jnp.einsum("kio,kbirc->borc", coarse_weight, terms1, precision=exact)
    act1 = jax.nn.softplus(pre1)
    pooled_count = nrows // 2 * lax.axis_size("face") * (ncols // 2) * lax.axis_size("tile")
    features = lax.psum(act1.sum(axis=(2, 3)), ("face", "tile")) / pooled_count
    hidden = jnp.tanh(
        jnp.dot(features, feature_weight, precision=exact)
        + jnp.dot(params, param_weight, precision=exact)
    )
    logits = jnp.dot(hidden, out_weight, precision=exact)
    dlogit = jax.nn.sigmoid(logits) - labels.astype(jnp.float32)
    dhidden = dlogit[:, None] * out_weight[None, :] * (1.0 - hidden * hidden)
    dfeatures = jnp.dot(dhidden, feature_weight.T, precision=exact)
    dpre1 = (dfeatures / pooled_count)[:, :, None, None] * jax.nn.sigmoid(pre1)
    grad_c = jnp.einsum("kbirc,borc->kio", terms1, dpre1, precision=exact)
    parts1 = jnp.einsum("kio,borc->kbirc", coarse_weight, dpre1, precision=exact)
    dfield1 = coarse_adjoint(parts1, flags)
    spread = jnp.broadcast_to(
        dfield1[:, :, :, None, :, None], (nmaps, nchan, nrows // 2, 2, ncols // 2, 2)
    ).reshape(pre0.shape)
    dpre0 = 0.25 * spread * jax.nn.sigmoid(pre0)
    grad_f = jnp.einsum("kbirc,borc->kio", terms0, dpre0, precision=exact)
    parts0 = jnp.einsum("kio,borc->kbirc", fine_weight, dpre0, precision=exact)
    inner0 = fine_apply(parts0[2], flags)
    outer0 = fine_apply(parts0[1] + 2.0 * inner0, flags)
    pixel_count = nrows * lax.axis_size("face") * ncols * lax.axis_size("tile")
    saliency = (parts0[0] - parts0[2] + outer0) * pixel_count
    grad_f, grad_c = lax.psum((grad_f, grad_c), ("face", "tile"))
    return (logits, saliency, grad_f, grad_c)


def solution(mesh):
    in_specs = (P(None, None, "face", "tile"), P(), P(), P(), P(), P(), P(), P(), P())
    out_specs = (P(), P(None, None, "face", "tile"), P(), P())
    return jax.shard_map(
        on_device, mesh=mesh, in_specs=in_specs, out_specs=out_specs, check_vma=False
    )
```

profile of v0, /device:TPU:0, one launch (start us, length us, event | category | flops | bytes accessed | tf_op | source)
XLA Modules:
  0.0 216.4 jit_solution(11895158124996952923)
XLA Ops:
  1.6 3.0 %collective-permute-start = (f32[4,4,1,128]{3,1,2,0:T(4,128)S(1)}, f32[4,4,1,128]{3,1,2,0:T(4,128)S(1)}, u32[]{:S(2)}, u32[]{:S(2)}) collective-permute-start(f32[4,4,1,128]{3,1,2,0:T(4,128)S(1)} %get-tuple-element.258), channel_id=1, source_target_pairs={{0,16},{16,0},{1,17},{17,1},{2,18},{18,2},{3,19},{19,3},{4,20},{20... | collective-permute-start | bytes 24584 | tf_op jit(solution)/shard_map/ppermute | solution.py:15
  8.5 4.4 %collective-permute-start.3 = (f32[4,4,18,1]{3,1,2,0:T(4,128)S(1)}, f32[4,4,18,1]{3,1,2,0:T(4,128)S(1)}, u32[]{:S(2)}, u32[]{:S(2)}) collective-permute-start(f32[4,4,18,1]{3,1,2,0:T(4,128)S(1)} %get-tuple-element.243), channel_id=1, source_target_pairs={{1,0},{2,1},{3,2},{4,3},{5,4},{6,5},{7,6},{8,7},{9,8},{10,9},{11,1... | collective-permute-start | bytes 3464 | tf_op jit(solution)/shard_map/ppermute | solution.py:18
  20.6 4.4 %collective-permute-start.7 = (f32[4,4,18,1]{3,1,2,0:T(4,128)S(1)}, f32[4,4,18,1]{3,1,2,0:T(4,128)S(1)}, u32[]{:S(2)}, u32[]{:S(2)}) collective-permute-start(f32[4,4,18,1]{3,1,2,0:T(4,128)S(1)} %get-tuple-element.241), channel_id=1, source_target_pairs={{1,0},{2,1},{3,2},{4,3},{5,4},{6,5},{7,6},{8,7},{9,8},{10,9},{11,1... | collective-permute-start | bytes 3464 | tf_op jit(solution)/shard_map/ppermute | solution.py:18
  29.0 1.7 compare_select_fusion.1
  30.7 2.6 %copy.39 = f32[4,16,16,128]{1,3,2,0:T(8,128)} copy(f32[4,16,16,128]{3,1,2,0:T(8,128)S(1)} %get-tuple-element.264) | data formatting | bytes 1048576 | tf_op jit(solution)/shard_map/jit(softplus)/select_n | solution.py:94
  33.3 5.6 %reduce_sum.18 = f32[4,16,8,64]{1,3,2,0:T(8,128)S(1)} reduce(f32[4,16,8,2,64,2]{1,5,4,3,2,0:T(2,128)} %bitcast.121, f32[]{:T(128)} %constant.420.clone.1), dimensions={3,5}, to_apply=%region_0.1 | reduce | flops 98304 | bytes 655364 | tf_op jit(solution)/shard_map/reduce_sum | solution.py:96
  39.3 1.6 collective-permute-start.8
  41.4 1.9 collective-permute-done.8
  45.1 4.4 %collective-permute-start.11 = (f32[4,16,10,1]{3,1,2,0:T(8,128)S(1)}, f32[4,16,10,1]{3,1,2,0:T(8,128)S(1)}, u32[]{:S(2)}, u32[]{:S(2)}) collective-permute-start(f32[4,16,10,1]{3,1,2,0:T(8,128)S(1)} %get-tuple-element.217), channel_id=1, source_target_pairs={{1,0},{2,1},{3,2},{4,3},{5,4},{6,5},{7,6},{8,7},{9,8},{10,9},{11,1... | collective-permute-start | bytes 7688 | tf_op jit(solution)/shard_map/ppermute | solution.py:18
  51.1 3.2 %collective-permute-done.10 = f32[4,16,10,1]{3,1,2,0:T(8,128)S(1)} collective-permute-done((f32[4,16,10,1]{3,1,2,0:T(8,128)S(1)}, f32[4,16,10,1]{3,1,2,0:T(8,128)S(1)}, u32[]{:S(2)}, u32[]{:S(2)}) %collective-permute-start.10) | collective-permute-done | bytes 2592 | tf_op jit(solution)/shard_map/ppermute | solution.py:15
  56.8 1.9 collective-permute-done.12
  59.4 4.4 %collective-permute-start.15 = (f32[4,16,10,1]{3,1,2,0:T(8,128)S(1)}, f32[4,16,10,1]{3,1,2,0:T(8,128)S(1)}, u32[]{:S(2)}, u32[]{:S(2)}) collective-permute-start(f32[4,16,10,1]{3,1,2,0:T(8,128)S(1)} %get-tuple-element.215), channel_id=1, source_target_pairs={{1,0},{2,1},{3,2},{4,3},{5,4},{6,5},{7,6},{8,7},{9,8},{10,9},{11,1... | collective-permute-start | bytes 7688 | tf_op jit(solution)/shard_map/ppermute | solution.py:18
  65.4 3.2 %collective-permute-done.14 = f32[4,16,10,1]{3,1,2,0:T(8,128)S(1)} collective-permute-done((f32[4,16,10,1]{3,1,2,0:T(8,128)S(1)}, f32[4,16,10,1]{3,1,2,0:T(8,128)S(1)}, u32[]{:S(2)}, u32[]{:S(2)}) %collective-permute-start.14) | collective-permute-done | bytes 2592 | tf_op jit(solution)/shard_map/ppermute | solution.py:15
  70.6 38.8 %psum.21 = f32[4,32]{1,0:T(4,128)S(1)} all-reduce(f32[4,32]{1,0:T(4,128)S(1)} %get-tuple-element.266), channel_id=1, replica_groups=mesh['face'=2,'tile'=16] {'face','tile'}, use_global_device_ids=true, to_apply=%region_2.3 | all-reduce | flops 128 | bytes 1024 | tf_op jit(solution)/shard_map/psum | solution.py:102
  111.6 2.3 %collective-permute-start.16 = (f32[4,16,1,64]{3,1,2,0:T(8,128)S(1)}, f32[4,16,1,64]{3,1,2,0:T(8,128)S(1)}, u32[]{:S(2)}, u32[]{:S(2)}) collective-permute-start(f32[4,16,1,64]{3,1,2,0:T(8,128)S(1)} %get-tuple-element.224), channel_id=1, source_target_pairs={{0,16},{16,0},{1,17},{17,1},{2,18},{18,2},{3,19},{19,3},{4,20},{20... | collective-permute-start | bytes 49160 | tf_op jit(solution)/shard_map/ppermute | solution.py:15
  114.0 2.0 collective-permute-done.16
  116.0 1.8 collective-permute-done.17
  118.7 4.4 %collective-permute-start.19 = (f32[4,16,10,1]{3,1,2,0:T(8,128)S(1)}, f32[4,16,10,1]{3,1,2,0:T(8,128)S(1)}, u32[]{:S(2)}, u32[]{:S(2)}) collective-permute-start(f32[4,16,10,1]{3,1,2,0:T(8,128)S(1)} %get-tuple-element.213), channel_id=1, source_target_pairs={{1,0},{2,1},{3,2},{4,3},{5,4},{6,5},{7,6},{8,7},{9,8},{10,9},{11,1... | collective-permute-start | bytes 7688 | tf_op jit(solution)/shard_map/ppermute | solution.py:18
  124.7 3.5 %collective-permute-done.18 = f32[4,16,10,1]{3,1,2,0:T(8,128)S(1)} collective-permute-done((f32[4,16,10,1]{3,1,2,0:T(8,128)}, f32[4,16,10,1]{3,1,2,0:T(8,128)S(1)}, u32[]{:S(2)}, u32[]{:S(2)}) %collective-permute-start.18) | collective-permute-done | bytes 2592 | tf_op jit(solution)/shard_map/ppermute | solution.py:15
  129.0 1.7 collective-permute-start.21
  130.7 1.9 collective-permute-done.20
  134.8 3.5 %collective-permute-start.23 = (f32[4,16,10,1]{3,1,2,0:T(8,128)S(1)}, f32[4,16,10,1]{3,1,2,0:T(8,128)S(1)}, u32[]{:S(2)}, u32[]{:S(2)}) collective-permute-start(f32[4,16,10,1]{3,1,2,0:T(8,128)S(1)} %get-tuple-element.211), channel_id=1, source_target_pairs={{1,0},{2,1},{3,2},{4,3},{5,4},{6,5},{7,6},{8,7},{9,8},{10,9},{11,1... | collective-permute-start | bytes 7688 | tf_op jit(solution)/shard_map/ppermute | solution.py:18
  139.8 3.5 %collective-permute-done.22 = f32[4,16,10,1]{3,1,2,0:T(8,128)S(1)} collective-permute-done((f32[4,16,10,1]{3,1,2,0:T(8,128)}, f32[4,16,10,1]{3,1,2,0:T(8,128)S(1)}, u32[]{:S(2)}, u32[]{:S(2)}) %collective-permute-start.22) | collective-permute-done | bytes 2592 | tf_op jit(solution)/shard_map/ppermute | solution.py:15
  144.0 4.0 %broadcast_in_dim.2 = f32[4,16,8,2,64,2]{1,5,4,3,2,0:T(2,128)} broadcast(f32[4,16,8,64]{1,3,2,0:T(8,128)S(1)} %copy.44), dimensions={0,1,2,4} | broadcast | bytes 655360 | tf_op jit(solution)/shard_map/broadcast_in_dim | solution.py:115
  148.0 2.8 %copy.45 = f32[4,16,16,128]{3,1,2,0:T(8,128)S(1)} copy(f32[4,16,16,128]{1,3,2,0:T(8,128)} %bitcast.120) | data formatting | bytes 1048576 | tf_op jit(solution)/shard_map/mul | solution.py:118
  151.8 1.7 collective-permute-start.24
  155.5 1.7 collective-permute-done.25
  158.8 3.0 %collective-permute-start.27 = (f32[4,4,18,1]{3,1,2,0:T(4,128)S(1)}, f32[4,4,18,1]{3,1,2,0:T(4,128)S(1)}, u32[]{:S(2)}, u32[]{:S(2)}) collective-permute-start(f32[4,4,18,1]{3,1,2,0:T(4,128)S(1)} %get-tuple-element.239), channel_id=1, source_target_pairs={{1,0},{2,1},{3,2},{4,3},{5,4},{6,5},{7,6},{8,7},{9,8},{10,9},{11,1... | collective-permute-start | bytes 3464 | tf_op jit(solution)/shard_map/ppermute | solution.py:18
  165.5 1.7 collective-permute-start.29
  167.2 1.7 convolution_bitcast_fusion.5
  168.9 39.0 %all-reduce = (f32[3,4,16]{2,1,0:T(4,128)}, f32[3,16,32]{2,1,0:T(8,128)}) all-reduce(f32[3,4,16]{2,1,0:T(4,128)S(1)} %convolution_bitcast_fusion.5, f32[3,16,32]{2,1,0:T(8,128)S(1)} %convolution_bitcast_fusion.4), channel_id=1, replica_groups=mesh['face'=2,'tile'=16] {'face','tile'}, use_global_device_ids=true, to_apply=%region_3.4 | all-reduce | flops 1728 | bytes 13824 | tf_op jit(solution)/shard_map/psum | solution.py:125
  208.1 4.4 %collective-permute-start.31 = (f32[4,4,18,1]{3,1,2,0:T(4,128)S(1)}, f32[4,4,18,1]{3,1,2,0:T(4,128)S(1)}, u32[]{:S(2)}, u32[]{:S(2)}) collective-permute-start(f32[4,4,18,1]{3,1,2,0:T(4,128)S(1)} %get-tuple-element.237), channel_id=1, source_target_pairs={{1,0},{2,1},{3,2},{4,3},{5,4},{6,5},{7,6},{8,7},{9,8},{10,9},{11,1... | collective-permute-start | bytes 3464 | tf_op jit(solution)/shard_map/ppermute | solution.py:18
  (161 shorter events, 49.1 us)
Async XLA Ops:
  1.6 5.2 %collective-permute-start = (f32[4,4,1,128]{3,1,2,0:T(4,128)S(1)}, f32[4,4,1,128]{3,1,2,0:T(4,128)S(1)}, u32[]{:S(2)}, u32[]{:S(2)}) collective-permute-start(f32[4,4,1,128]{3,1,2,0:T(4,128)S(1)} %get-tuple-element.258), channel_id=1, source_target_pairs={{0,16},{16,0},{1,17},{17,1},{2,18},{18,2},{3,19},{19,3},{4,20},{20... | collective-permute-start | bytes 24584 | tf_op jit(solution)/shard_map/ppermute | solution.py:15
  4.6 3.7 %collective-permute-start.1 = (f32[4,4,1,128]{3,1,2,0:T(4,128)S(1)}, f32[4,4,1,128]{3,1,2,0:T(4,128)S(1)}, u32[]{:S(2)}, u32[]{:S(2)}) collective-permute-start(f32[4,4,1,128]{3,1,2,0:T(4,128)S(1)} %get-tuple-element.259), channel_id=1, source_target_pairs={{16,0},{0,16},{17,1},{1,17},{18,2},{2,18},{19,3},{3,19},{20,4},{4,... | collective-permute-start | bytes 24584 | tf_op jit(solution)/shard_map/ppermute | solution.py:18
  8.4 7.4 %collective-permute-start.2 = (f32[4,4,18,1]{3,1,2,0:T(4,128)S(1)}, f32[4,4,18,1]{3,1,2,0:T(4,128)S(1)}, u32[]{:S(2)}, u32[]{:S(2)}) collective-permute-start(f32[4,4,18,1]{3,1,2,0:T(4,128)S(1)} %get-tuple-element.242), channel_id=1, source_target_pairs={{0,1},{1,2},{2,3},{3,4},{4,5},{5,6},{6,7},{7,8},{8,9},{9,10},{10,1... | collective-permute-start | bytes 3464 | tf_op jit(solution)/shard_map/ppermute | solution.py:15
  8.5 7.4 %collective-permute-start.3 = (f32[4,4,18,1]{3,1,2,0:T(4,128)S(1)}, f32[4,4,18,1]{3,1,2,0:T(4,128)S(1)}, u32[]{:S(2)}, u32[]{:S(2)}) collective-permute-start(f32[4,4,18,1]{3,1,2,0:T(4,128)S(1)} %get-tuple-element.243), channel_id=1, source_target_pairs={{1,0},{2,1},{3,2},{4,3},{5,4},{6,5},{7,6},{8,7},{9,8},{10,9},{11,1... | collective-permute-start | bytes 3464 | tf_op jit(solution)/shard_map/ppermute | solution.py:18
  16.1 3.7 %collective-permute-start.4 = (f32[4,4,1,128]{3,1,2,0:T(4,128)S(1)}, f32[4,4,1,128]{3,1,2,0:T(4,128)S(1)}, u32[]{:S(2)}, u32[]{:S(2)}) collective-permute-start(f32[4,4,1,128]{3,1,2,0:T(4,128)S(1)} %get-tuple-element.254), channel_id=1, source_target_pairs={{0,16},{16,0},{1,17},{17,1},{2,18},{18,2},{3,19},{19,3},{4,20},{20... | collective-permute-start | bytes 24584 | tf_op jit(solution)/shard_map/ppermute | solution.py:15
  16.7 3.7 %collective-permute-start.5 = (f32[4,4,1,128]{3,1,2,0:T(4,128)S(1)}, f32[4,4,1,128]{3,1,2,0:T(4,128)S(1)}, u32[]{:S(2)}, u32[]{:S(2)}) collective-permute-start(f32[4,4,1,128]{3,1,2,0:T(4,128)S(1)} %get-tuple-element.255), channel_id=1, source_target_pairs={{16,0},{0,16},{17,1},{1,17},{18,2},{2,18},{19,3},{3,19},{20,4},{4,... | collective-permute-start | bytes 24584 | tf_op jit(solution)/shard_map/ppermute | solution.py:18
  20.5 7.3 %collective-permute-start.6 = (f32[4,4,18,1]{3,1,2,0:T(4,128)S(1)}, f32[4,4,18,1]{3,1,2,0:T(4,128)S(1)}, u32[]{:S(2)}, u32[]{:S(2)}) collective-permute-start(f32[4,4,18,1]{3,1,2,0:T(4,128)S(1)} %get-tuple-element.240), channel_id=1, source_target_pairs={{0,1},{1,2},{2,3},{3,4},{4,5},{5,6},{6,7},{7,8},{8,9},{9,10},{10,1... | collective-permute-start | bytes 3464 | tf_op jit(solution)/shard_map/ppermute | solution.py:15
  20.6 7.3 %collective-permute-start.7 = (f32[4,4,18,1]{3,1,2,0:T(4,128)S(1)}, f32[4,4,18,1]{3,1,2,0:T(4,128)S(1)}, u32[]{:S(2)}, u32[]{:S(2)}) collective-permute-start(f32[4,4,18,1]{3,1,2,0:T(4,128)S(1)} %get-tuple-element.241), channel_id=1, source_target_pairs={{1,0},{2,1},{3,2},{4,3},{5,4},{6,5},{7,6},{8,7},{9,8},{10,9},{11,1... | collective-permute-start | bytes 3464 | tf_op jit(solution)/shard_map/ppermute | solution.py:18
  39.3 4.0 %collective-permute-start.8 = (f32[4,16,1,64]{3,1,2,0:T(8,128)S(1)}, f32[4,16,1,64]{3,1,2,0:T(8,128)S(1)}, u32[]{:S(2)}, u32[]{:S(2)}) collective-permute-start(f32[4,16,1,64]{3,1,2,0:T(8,128)S(1)} %get-tuple-element.234), channel_id=1, source_target_pairs={{0,16},{16,0},{1,17},{17,1},{2,18},{18,2},{3,19},{19,3},{4,20},{20... | collective-permute-start | bytes 49160 | tf_op jit(solution)/shard_map/ppermute | solution.py:15
  41.0 3.9 %collective-permute-start.9 = (f32[4,16,1,64]{3,1,2,0:T(8,128)S(1)}, f32[4,16,1,64]{3,1,2,0:T(8,128)S(1)}, u32[]{:S(2)}, u32[]{:S(2)}) collective-permute-start(f32[4,16,1,64]{3,1,2,0:T(8,128)S(1)} %get-tuple-element.235), channel_id=1, source_target_pairs={{16,0},{0,16},{17,1},{1,17},{18,2},{2,18},{19,3},{3,19},{20,4},{4,... | collective-permute-start | bytes 49160 | tf_op jit(solution)/shard_map/ppermute | solution.py:18
  45.1 9.2 %collective-permute-start.10 = (f32[4,16,10,1]{3,1,2,0:T(8,128)S(1)}, f32[4,16,10,1]{3,1,2,0:T(8,128)S(1)}, u32[]{:S(2)}, u32[]{:S(2)}) collective-permute-start(f32[4,16,10,1]{3,1,2,0:T(8,128)S(1)} %get-tuple-element.216), channel_id=1, source_target_pairs={{0,1},{1,2},{2,3},{3,4},{4,5},{5,6},{6,7},{7,8},{8,9},{9,10},{10,1... | collective-permute-start | bytes 7688 | tf_op jit(solution)/shard_map/ppermute | solution.py:15
  45.1 9.2 %collective-permute-start.11 = (f32[4,16,10,1]{3,1,2,0:T(8,128)S(1)}, f32[4,16,10,1]{3,1,2,0:T(8,128)S(1)}, u32[]{:S(2)}, u32[]{:S(2)}) collective-permute-start(f32[4,16,10,1]{3,1,2,0:T(8,128)S(1)} %get-tuple-element.217), channel_id=1, source_target_pairs={{1,0},{2,1},{3,2},{4,3},{5,4},{6,5},{7,6},{8,7},{9,8},{10,9},{11,1... | collective-permute-start | bytes 7688 | tf_op jit(solution)/shard_map/ppermute | solution.py:18
  54.7 4.0 %collective-permute-start.12 = (f32[4,16,1,64]{3,1,2,0:T(8,128)S(1)}, f32[4,16,1,64]{3,1,2,0:T(8,128)S(1)}, u32[]{:S(2)}, u32[]{:S(2)}) collective-permute-start(f32[4,16,1,64]{3,1,2,0:T(8,128)S(1)} %get-tuple-element.230), channel_id=1, source_target_pairs={{0,16},{16,0},{1,17},{17,1},{2,18},{18,2},{3,19},{19,3},{4,20},{20... | collective-permute-start | bytes 49160 | tf_op jit(solution)/shard_map/ppermute | solution.py:15
  55.2 3.9 %collective-permute-start.13 = (f32[4,16,1,64]{3,1,2,0:T(8,128)S(1)}, f32[4,16,1,64]{3,1,2,0:T(8,128)S(1)}, u32[]{:S(2)}, u32[]{:S(2)}) collective-permute-start(f32[4,16,1,64]{3,1,2,0:T(8,128)S(1)} %get-tuple-element.231), channel_id=1, source_target_pairs={{16,0},{0,16},{17,1},{1,17},{18,2},{2,18},{19,3},{3,19},{20,4},{4,... | collective-permute-start | bytes 49160 | tf_op jit(solution)/shard_map/ppermute | solution.py:18
  59.3 9.2 %collective-permute-start.14 = (f32[4,16,10,1]{3,1,2,0:T(8,128)S(1)}, f32[4,16,10,1]{3,1,2,0:T(8,128)S(1)}, u32[]{:S(2)}, u32[]{:S(2)}) collective-permute-start(f32[4,16,10,1]{3,1,2,0:T(8,128)S(1)} %get-tuple-element.214), channel_id=1, source_target_pairs={{0,1},{1,2},{2,3},{3,4},{4,5},{5,6},{6,7},{7,8},{8,9},{9,10},{10,1... | collective-permute-start | bytes 7688 | tf_op jit(solution)/shard_map/ppermute | solution.py:15
  59.4 9.2 %collective-permute-start.15 = (f32[4,16,10,1]{3,1,2,0:T(8,128)S(1)}, f32[4,16,10,1]{3,1,2,0:T(8,128)S(1)}, u32[]{:S(2)}, u32[]{:S(2)}) collective-permute-start(f32[4,16,10,1]{3,1,2,0:T(8,128)S(1)} %get-tuple-element.215), channel_id=1, source_target_pairs={{1,0},{2,1},{3,2},{4,3},{5,4},{6,5},{7,6},{8,7},{9,8},{10,9},{11,1... | collective-permute-start | bytes 7688 | tf_op jit(solution)/shard_map/ppermute | solution.py:18
  111.6 4.4 %collective-permute-start.16 = (f32[4,16,1,64]{3,1,2,0:T(8,128)S(1)}, f32[4,16,1,64]{3,1,2,0:T(8,128)S(1)}, u32[]{:S(2)}, u32[]{:S(2)}) collective-permute-start(f32[4,16,1,64]{3,1,2,0:T(8,128)S(1)} %get-tuple-element.224), channel_id=1, source_target_pairs={{0,16},{16,0},{1,17},{17,1},{2,18},{18,2},{3,19},{19,3},{4,20},{20... | collective-permute-start | bytes 49160 | tf_op jit(solution)/shard_map/ppermute | solution.py:15
  113.9 3.9 %collective-permute-start.17 = (f32[4,16,1,64]{3,1,2,0:T(8,128)S(1)}, f32[4,16,1,64]{3,1,2,0:T(8,128)S(1)}, u32[]{:S(2)}, u32[]{:S(2)}) collective-permute-start(f32[4,16,1,64]{3,1,2,0:T(8,128)S(1)} %get-tuple-element.225), channel_id=1, source_target_pairs={{16,0},{0,16},{17,1},{1,17},{18,2},{2,18},{19,3},{3,19},{20,4},{4,... | collective-permute-start | bytes 49160 | tf_op jit(solution)/shard_map/ppermute | solution.py:18
  118.7 9.5 %collective-permute-start.18 = (f32[4,16,10,1]{3,1,2,0:T(8,128)}, f32[4,16,10,1]{3,1,2,0:T(8,128)S(1)}, u32[]{:S(2)}, u32[]{:S(2)}) collective-permute-start(f32[4,16,10,1]{3,1,2,0:T(8,128)} %get-tuple-element.212), channel_id=1, source_target_pairs={{0,1},{1,2},{2,3},{3,4},{4,5},{5,6},{6,7},{7,8},{8,9},{9,10},{10,1... | collective-permute-start | bytes 7688 | tf_op jit(solution)/shard_map/ppermute | solution.py:15
  118.7 9.5 %collective-permute-start.19 = (f32[4,16,10,1]{3,1,2,0:T(8,128)S(1)}, f32[4,16,10,1]{3,1,2,0:T(8,128)S(1)}, u32[]{:S(2)}, u32[]{:S(2)}) collective-permute-start(f32[4,16,10,1]{3,1,2,0:T(8,128)S(1)} %get-tuple-element.213), channel_id=1, source_target_pairs={{1,0},{2,1},{3,2},{4,3},{5,4},{6,5},{7,6},{8,7},{9,8},{10,9},{11,1... | collective-permute-start | bytes 7688 | tf_op jit(solution)/shard_map/ppermute | solution.py:18
  128.6 4.0 %collective-permute-start.20 = (f32[4,16,1,64]{3,1,2,0:T(8,128)S(1)}, f32[4,16,1,64]{3,1,2,0:T(8,128)S(1)}, u32[]{:S(2)}, u32[]{:S(2)}) collective-permute-start(f32[4,16,1,64]{3,1,2,0:T(8,128)S(1)} %get-tuple-element.220), channel_id=1, source_target_pairs={{0,16},{16,0},{1,17},{17,1},{2,18},{18,2},{3,19},{19,3},{4,20},{20... | collective-permute-start | bytes 49160 | tf_op jit(solution)/shard_map/ppermute | solution.py:15
  129.0 3.9 %collective-permute-start.21 = (f32[4,16,1,64]{3,1,2,0:T(8,128)S(1)}, f32[4,16,1,64]{3,1,2,0:T(8,128)S(1)}, u32[]{:S(2)}, u32[]{:S(2)}) collective-permute-start(f32[4,16,1,64]{3,1,2,0:T(8,128)S(1)} %get-tuple-element.221), channel_id=1, source_target_pairs={{16,0},{0,16},{17,1},{1,17},{18,2},{2,18},{19,3},{3,19},{20,4},{4,... | collective-permute-start | bytes 49160 | tf_op jit(solution)/shard_map/ppermute | solution.py:18
  133.8 9.5 %collective-permute-start.22 = (f32[4,16,10,1]{3,1,2,0:T(8,128)}, f32[4,16,10,1]{3,1,2,0:T(8,128)S(1)}, u32[]{:S(2)}, u32[]{:S(2)}) collective-permute-start(f32[4,16,10,1]{3,1,2,0:T(8,128)} %get-tuple-element.210), channel_id=1, source_target_pairs={{0,1},{1,2},{2,3},{3,4},{4,5},{5,6},{6,7},{7,8},{8,9},{9,10},{10,1... | collective-permute-start | bytes 7688 | tf_op jit(solution)/shard_map/ppermute | solution.py:15
  134.8 8.5 %collective-permute-start.23 = (f32[4,16,10,1]{3,1,2,0:T(8,128)S(1)}, f32[4,16,10,1]{3,1,2,0:T(8,128)S(1)}, u32[]{:S(2)}, u32[]{:S(2)}) collective-permute-start(f32[4,16,10,1]{3,1,2,0:T(8,128)S(1)} %get-tuple-element.211), channel_id=1, source_target_pairs={{1,0},{2,1},{3,2},{4,3},{5,4},{6,5},{7,6},{8,7},{9,8},{10,9},{11,1... | collective-permute-start | bytes 7688 | tf_op jit(solution)/shard_map/ppermute | solution.py:18
  151.8 3.7 %collective-permute-start.24 = (f32[4,4,1,128]{3,1,2,0:T(4,128)S(1)}, f32[4,4,1,128]{3,1,2,0:T(4,128)S(1)}, u32[]{:S(2)}, u32[]{:S(2)}) collective-permute-start(f32[4,4,1,128]{3,1,2,0:T(4,128)S(1)} %get-tuple-element.250), channel_id=1, source_target_pairs={{0,16},{16,0},{1,17},{17,1},{2,18},{18,2},{3,19},{19,3},{4,20},{20... | collective-permute-start | bytes 24584 | tf_op jit(solution)/shard_map/ppermute | solution.py:15
  153.5 3.7 %collective-permute-start.25 = (f32[4,4,1,128]{3,1,2,0:T(4,128)S(1)}, f32[4,4,1,128]{3,1,2,0:T(4,128)S(1)}, u32[]{:S(2)}, u32[]{:S(2)}) collective-permute-start(f32[4,4,1,128]{3,1,2,0:T(4,128)S(1)} %get-tuple-element.251), channel_id=1, source_target_pairs={{16,0},{0,16},{17,1},{1,17},{18,2},{2,18},{19,3},{3,19},{20,4},{4,... | collective-permute-start | bytes 24584 | tf_op jit(solution)/shard_map/ppermute | solution.py:18
  157.4 7.4 %collective-permute-start.26 = (f32[4,4,18,1]{3,1,2,0:T(4,128)S(1)}, f32[4,4,18,1]{3,1,2,0:T(4,128)S(1)}, u32[]{:S(2)}, u32[]{:S(2)}) collective-permute-start(f32[4,4,18,1]{3,1,2,0:T(4,128)S(1)} %get-tuple-element.238), channel_id=1, source_target_pairs={{0,1},{1,2},{2,3},{3,4},{4,5},{5,6},{6,7},{7,8},{8,9},{9,10},{10,1... | collective-permute-start | bytes 3464 | tf_op jit(solution)/shard_map/ppermute | solution.py:15
  158.8 6.0 %collective-permute-start.27 = (f32[4,4,18,1]{3,1,2,0:T(4,128)S(1)}, f32[4,4,18,1]{3,1,2,0:T(4,128)S(1)}, u32[]{:S(2)}, u32[]{:S(2)}) collective-permute-start(f32[4,4,18,1]{3,1,2,0:T(4,128)S(1)} %get-tuple-element.239), channel_id=1, source_target_pairs={{1,0},{2,1},{3,2},{4,3},{5,4},{6,5},{7,6},{8,7},{9,8},{10,9},{11,1... | collective-permute-start | bytes 3464 | tf_op jit(solution)/shard_map/ppermute | solution.py:18
  165.1 42.8 %collective-permute-start.28 = (f32[4,4,1,128]{3,1,2,0:T(4,128)S(1)}, f32[4,4,1,128]{3,1,2,0:T(4,128)S(1)}, u32[]{:S(2)}, u32[]{:S(2)}) collective-permute-start(f32[4,4,1,128]{3,1,2,0:T(4,128)S(1)} %get-tuple-element.246), channel_id=1, source_target_pairs={{0,16},{16,0},{1,17},{17,1},{2,18},{18,2},{3,19},{19,3},{4,20},{20... | collective-permute-start | bytes 24584 | tf_op jit(solution)/shard_map/ppermute | solution.py:15
  165.5 42.3 %collective-permute-start.29 = (f32[4,4,1,128]{3,1,2,0:T(4,128)S(1)}, f32[4,4,1,128]{3,1,2,0:T(4,128)S(1)}, u32[]{:S(2)}, u32[]{:S(2)}) collective-permute-start(f32[4,4,1,128]{3,1,2,0:T(4,128)S(1)} %get-tuple-element.247), channel_id=1, source_target_pairs={{16,0},{0,16},{17,1},{1,17},{18,2},{2,18},{19,3},{3,19},{20,4},{4,... | collective-permute-start | bytes 24584 | tf_op jit(solution)/shard_map/ppermute | solution.py:18
  208.0 7.4 %collective-permute-start.30 = (f32[4,4,18,1]{3,1,2,0:T(4,128)S(1)}, f32[4,4,18,1]{3,1,2,0:T(4,128)S(1)}, u32[]{:S(2)}, u32[]{:S(2)}) collective-permute-start(f32[4,4,18,1]{3,1,2,0:T(4,128)S(1)} %get-tuple-element.236), channel_id=1, source_target_pairs={{0,1},{1,2},{2,3},{3,4},{4,5},{5,6},{6,7},{7,8},{8,9},{9,10},{10,1... | collective-permute-start | bytes 3464 | tf_op jit(solution)/shard_map/ppermute | solution.py:15
  208.1 7.4 %collective-permute-start.31 = (f32[4,4,18,1]{3,1,2,0:T(4,128)S(1)}, f32[4,4,18,1]{3,1,2,0:T(4,128)S(1)}, u32[]{:S(2)}, u32[]{:S(2)}) collective-permute-start(f32[4,4,18,1]{3,1,2,0:T(4,128)S(1)} %get-tuple-element.237), channel_id=1, source_target_pairs={{1,0},{2,1},{3,2},{4,3},{5,4},{6,5},{7,6},{8,7},{9,8},{10,9},{11,1... | collective-permute-start | bytes 3464 | tf_op jit(solution)/shard_map/ppermute | solution.py:18
  (16 other events, 461.8 us)
where the time goes:
time: 218 us; the launch traced here: 216 us
  blocking collectives  77.8 us (36%)
  starting transfers between devices  53.9 us (25%)
  waiting for transfers between devices  36.5 us (17%)
  other arithmetic  21.7 us (10%)
  local copies, waits for them, and re-layouts  17 us (8%)
  matrix products  8.29 us (4%)
    ppermute x16, starting transfers between devices, with_halo(): lax.ppermute(lax.slice_in_dim(block, 0, width, axis=dim), axis, backward)  40.5 us
    psum x1, blocking collectives, on_device(): grad_f, grad_c = lax.psum((grad_f, grad_c), ('face', 'tile'))  39 us
    psum x1, blocking collectives, on_device(): features = lax.psum(act1.sum(axis=(2, 3)), ('face', 'tile')) / pooled_count  38.8 us
    ppermute x16, waiting for transfers between devices, with_halo(): lax.ppermute(lax.slice_in_dim(block, block.shape[dim] - width, None, axis...  28.7 us
    ppermute x16, starting transfers between devices, with_halo(): lax.ppermute(lax.slice_in_dim(block, block.shape[dim] - width, None, axis...  13.3 us
    ppermute x16, waiting for transfers between devices, with_halo(): lax.ppermute(lax.slice_in_dim(block, 0, width, axis=dim), axis, backward)  7.84 us
    scatter x8, other arithmetic, stencil(): lower.at[..., -1, :]  6.22 us
    reduce_sum x1, other arithmetic, on_device(): act0.reshape(nmaps, nchan, nrows // 2, 2, ncols // 2, 2).mean(axis=(3, 5))  5.64 us
  transfers between devices with their start and end apart: 32, of which 21 were waited for; matrix products, arithmetic and copies ran while one was open for 8% of the time, Pallas kernels for 0%

commit v1 on v0

v1 whole, which is shorter than its diff:
```python
import functools

import jax
import jax.numpy as jnp
from jax import lax
from jax.experimental import pallas as pl
from jax.experimental.pallas import tpu as pltpu
from jax.sharding import PartitionSpec as P

f32 = jnp.float32
exact = lax.Precision.HIGHEST
MESH = pl.DeviceIdType.MESH
LANES = 128
HALF = 64
UP, DOWN, LEFT, RIGHT, UL, UR, DL, DR = range(8)


def mm(a, b, ca=1, cb=0, precision=exact):
    return lax.dot_general(
        a, b, (((ca,), (cb,)), ((), ())), precision=precision, preferred_element_type=f32
    )


def iota(shape, dim):
    return lax.broadcasted_iota(jnp.int32, shape, dim)


def onehot(cond):
    return jnp.where(cond, 1.0, 0.0).astype(f32)


def swap(x):
    return pltpu.roll(x, HALF, axis=x.ndim - 1)


def pick(flag, yes, no):
    return flag * yes + (1.0 - flag) * no


def from_left(x, edge):
    axis = x.ndim - 2
    return jnp.where(iota(x.shape, axis) == 0, edge, pltpu.roll(x, 1, axis=axis))


def from_right(x, edge):
    axis = x.ndim - 2
    n = x.shape[axis]
    return jnp.where(iota(x.shape, axis) == n - 1, edge, pltpu.roll(x, n - 1, axis=axis))


def beside(x, left, right, fine):
    if not fine:
        return from_left(x, left) + from_right(x, right)
    s = swap(x)
    even = iota(x.shape, x.ndim - 1) < HALF
    return s + jnp.where(even, from_left(s, swap(left)), from_right(s, swap(right)))


def lap(x, up, down, left, right, fine):
    above = jnp.concatenate([up[None], x[:-1]], axis=0)
    below = jnp.concatenate([x[1:], down[None]], axis=0)
    return -0.25 * (above + below + beside(x, left, right, fine))


class Exchange:
    def __init__(self, field, bufs, send_sem, recv_sem, place, fine):
        self.field, self.place, self.fine = field, place, fine
        self.row_recv, self.col_send, self.col_recv, self.end_send, self.end_recv = bufs
        self.send_sem, self.recv_sem = send_sem, recv_sem

    def start(self):
        field, (face, tile, faces, tiles) = self.field, self.place
        nrows, ncols, _ = field.shape
        up, down = lax.rem(face + faces - 1, faces), lax.rem(face + 1, faces)
        left, right = lax.rem(tile + tiles - 1, tiles), lax.rem(tile + 1, tiles)
        copies = [None] * 8

        def send(way, src, dst, target):
            copies[way] = pltpu.make_async_remote_copy(
                src_ref=src,
                dst_ref=dst,
                send_sem=self.send_sem.at[way],
                recv_sem=self.recv_sem.at[way],
                device_id=target,
                device_id_type=MESH,
            )
            copies[way].start()

        send(UP, field.at[pl.ds(0, 2)], self.row_recv.at[1], (up, tile))
        send(DOWN, field.at[pl.ds(nrows - 2, 2)], self.row_recv.at[0], (down, tile))
        width = self.col_send.shape[1]
        for w in range(width):
            self.col_send[0, w] = field[:, w : w + 1, :]
            self.col_send[1, w] = field[:, ncols - 1 - w : ncols - w, :]
        for side, row in ((0, 0), (1, nrows - 1)):
            self.end_send[side, 0] = field[row, 0:1, :]
            self.end_send[side, 1] = field[row, ncols - 1 : ncols, :]
        send(LEFT, self.col_send.at[0], self.col_recv.at[1], (face, left))
        send(RIGHT, self.col_send.at[1], self.col_recv.at[0], (face, right))
        send(UL, self.end_send.at[0], self.end_recv.at[3], (up, left))
        send(UR, self.end_send.at[0], self.end_recv.at[2], (up, right))
        send(DL, self.end_send.at[1], self.end_recv.at[1], (down, left))
        send(DR, self.end_send.at[1], self.end_recv.at[0], (down, right))
        self.copies = copies

    def turn(self, x):
        return swap(x) if self.fine else x

    def outer(self, flags, rows, end_left, end_right):
        flag_left, flag, flag_right = flags
        ncols = rows.shape[1]
        mirror = onehot(iota((ncols, ncols), 0) + iota((ncols, ncols), 1) == ncols - 1)
        pair = jnp.concatenate([rows[0], rows[1]], axis=1)
        turned = mm(mirror, pair)
        rows = [
            pick(flag, self.turn(turned[:, LANES * i : LANES * (i + 1)]), rows[i]) for i in range(2)
        ]
        row_left = pick(flag, self.turn(end_right[0]), end_left[1])
        row_right = pick(flag, self.turn(end_left[1]), end_right[0])
        col_left = pick(flag_left, self.turn(end_left[0]), end_left[1])
        col_right = pick(flag_right, self.turn(end_right[1]), end_right[0])
        return rows, row_left, row_right, col_left, col_right

    def finish(self, flags_up, flags_down):
        for copy in self.copies:
            copy.wait()
        fine = self.fine
        x = self.field[...]
        nrows, ncols, _ = x.shape
        ends = self.end_recv[...]
        (u2, u1), ul, ur, lu, ru = self.outer(flags_up, self.row_recv[0], ends[0], ends[1])
        (d1, d2), dl, dr, ld, rd = self.outer(flags_down, self.row_recv[1], ends[2], ends[3])
        lefts, rights = self.col_recv[0], self.col_recv[1]
        first = lap(x, u1, d1, lefts[0], rights[0], fine)
        first_u = -0.25 * (u2 + x[0] + beside(u1, ul, ur, fine))
        first_d = -0.25 * (d2 + x[nrows - 1] + beside(d1, dl, dr, fine))
        if fine:
            along_l = swap(lefts[0]) + swap(self.field[:, 0:1, :])
            along_r = swap(rights[0]) + swap(self.field[:, ncols - 1 : ncols, :])
        else:
            along_l = lefts[1] + self.field[:, 0:1, :]
            along_r = rights[1] + self.field[:, ncols - 1 : ncols, :]

        def edge(col, over, under, along):
            above = jnp.concatenate([over[None], col[:-1]], axis=0)
            below = jnp.concatenate([col[1:], under[None]], axis=0)
            return -0.25 * (above + below + along)

        first_l = edge(lefts[0], lu, ld, along_l)
        first_r = edge(rights[0], ru, rd, along_r)
        second = 2.0 * lap(first, first_u, first_d, first_l, first_r, fine) - x
        return first, second


class GroupSum:
    def __init__(self, slots, sems, me, device_of):
        self.slots, self.sems, self.me, self.device_of = slots, sems, me, device_of
        self.count = slots.shape[0]

    def start(self, value):
        me, count = self.me, self.count
        self.slots[me] = value

        def step(k, _):
            pltpu.make_async_remote_copy(
                src_ref=self.slots.at[me],
                dst_ref=self.slots.at[me],
                send_sem=self.sems.at[0],
                recv_sem=self.sems.at[1],
                device_id=self.device_of(lax.rem(me + k, count)),
                device_id_type=MESH,
            ).start()
            return 0

        lax.fori_loop(1, count, step, 0)

    def finish(self):
        others = self.slots.at[pl.ds(0, self.count - 1)]
        pltpu.make_async_copy(others, others, self.sems.at[1]).wait()
        pltpu.make_async_copy(others, others, self.sems.at[0]).wait()
        total = self.slots[0]
        if self.count <= 8:
            for i in range(1, self.count):
                total = total + self.slots[i]
            return total
        return jnp.sum(self.slots[...], axis=0)


def kernel(
    faces,
    tiles,
    maps_ref,
    params_ref,
    labels_ref,
    flip_ref,
    fine_ref,
    coarse_ref,
    feature_ref,
    param_w_ref,
    out_w_ref,
    logits_ref,
    sal_ref,
    grad_f_ref,
    grad_c_ref,
    x0_ref,
    t0_ref,
    sig0_ref,
    x1_ref,
    t1_ref,
    d1_ref,
    d0_ref,
    sal_t_ref,
    fine_rows,
    fine_col_send,
    fine_col_recv,
    coarse_rows,
    coarse_col_send,
    coarse_col_recv,
    end_send,
    end_recv,
    halo_send,
    halo_recv,
    feature_slots,
    face_slots,
    low_slots,
    high_slots,
    sum_sems,
):
    face, tile = lax.axis_index("face"), lax.axis_index("tile")
    place = (face, tile, faces, tiles)
    devices = faces * tiles
    linear = face * tiles + tile
    nbins, nch0 = fine_ref.shape[1:]
    nch1 = coarse_ref.shape[2]
    nmaps = params_ref.shape[0]
    order = fine_ref.shape[0]
    nrows = maps_ref.shape[0]
    ncols = maps_ref.shape[2] // 2
    fields = nmaps * nbins
    pooled = float(nrows // 2 * ncols * devices)

    def device_of(i):
        return (lax.div(i, tiles), lax.rem(i, tiles))

    barrier = pltpu.get_barrier_semaphore()

    def greet(k, _):
        pl.semaphore_signal(
            barrier,
            inc=1,
            device_id=device_of(lax.rem(linear + k, devices)),
            device_id_type=MESH,
        )
        return 0

    lax.fori_loop(1, devices, greet, 0)

    col = iota((ncols, 2 * ncols), 1)
    pairs = [
        onehot(col == 2 * iota((ncols, 2 * ncols), 0) + p).astype(jnp.bfloat16) for p in range(2)
    ]

    zero = jnp.zeros((HALF - fields, 2 * ncols), jnp.bfloat16)

    def load_row(r, _):
        row = jnp.concatenate([maps_ref[r], zero], axis=0)
        halves = [mm(pairs[p], row, 1, 1, None) for p in range(2)]
        x0_ref[r] = jnp.concatenate(halves, axis=1)
        return 0

    lax.fori_loop(0, nrows, load_row, 0)
    pl.semaphore_wait(barrier, devices - 1)

    def exchange(i, field, fine):
        rows, sends, recvs = (
            (fine_rows, fine_col_send, fine_col_recv)
            if fine
            else (coarse_rows, coarse_col_send, coarse_col_recv)
        )
        slot = i // 2
        bufs = (rows.at[slot], sends.at[slot], recvs.at[slot], end_send.at[i], end_recv.at[i])
        return Exchange(field, bufs, halo_send.at[i], halo_recv.at[i], place, fine)

    ex0 = exchange(0, x0_ref, True)
    ex0.start()

    below = lax.rem(face + 1, faces)
    spots = (lax.rem(tile + tiles - 1, tiles), tile, lax.rem(tile + 1, tiles))
    flags_up = [jnp.where(flip_ref[face, s] == 1, 1.0, 0.0).astype(f32) for s in spots]
    flags_down = [jnp.where(flip_ref[below, s] == 1, 1.0, 0.0).astype(f32) for s in spots]

    square = (LANES, LANES)
    ri, ci = iota(square, 0), iota(square, 1)
    mask0 = onehot(
        (ri // HALF == ci // HALF)
        & (ri % HALF < fields)
        & ((ri % HALF) // nbins == (ci % HALF) // nch0)
    )
    mask1 = onehot((ri % HALF) // nch0 == ci // nch1)
    at_bin = onehot(iota((LANES, nbins), 0) % nbins == iota((LANES, nbins), 1))
    at_ch0 = onehot(iota((nch0, LANES), 1) % nch0 == iota((nch0, LANES), 0))
    at_ch1 = onehot(iota((nch1, LANES), 1) % nch1 == iota((nch1, LANES), 0))
    w0 = [mask0 * mm(mm(at_bin, fine_ref[k]), at_ch0) for k in range(order)]
    w1 = [mask1 * mm(mm(at_ch0, coarse_ref[k], 0, 0), at_ch1) for k in range(order)]
    wf = mm(at_ch1, feature_ref[...], 0, 0)
    head_mask = onehot(iota((nmaps, LANES), 0) == iota((nmaps, LANES), 1) // nch1)

    first, second = ex0.finish(flags_up, flags_down)
    t0_ref[0] = first
    t0_ref[1] = second

    def flat(x):
        return x.reshape(-1, LANES)

    def conv(terms, weights, cb):
        total = mm(flat(terms[0]), weights[0], 1, cb)
        for k in range(1, order):
            total = total + mm(flat(terms[k]), weights[k], 1, cb)
        return total

    pre0 = conv((x0_ref[...], first, second), w0, 0)
    small = jnp.exp(-jnp.abs(pre0))
    act0 = jnp.maximum(pre0, 0.0) + jnp.log1p(small)
    sig0_ref[...] = (0.25 * jnp.where(pre0 >= 0, 1.0, small) / (1.0 + small)).reshape(
        nrows, ncols, LANES
    )
    act0 = act0.reshape(nrows // 2, 2, ncols, LANES)
    x1_ref[...] = 0.25 * (act0[:, 0] + act0[:, 1])

    ex1 = exchange(1, x1_ref, False)
    ex1.start()
    first, second = ex1.finish(flags_up, flags_down)
    t1_ref[0] = first
    t1_ref[1] = second
    pre1 = conv((x1_ref[...], first, second), w1, 0)
    small = jnp.exp(-jnp.abs(pre1))
    act1 = jnp.maximum(pre1, 0.0) + jnp.log1p(small)
    feature_sum = GroupSum(feature_slots, sum_sems.at[0], linear, device_of)
    feature_sum.start(jnp.sum(act1, axis=0, keepdims=True))
    sig1 = jnp.where(pre1 >= 0, 1.0, small) / (1.0 + small)
    from_params = params_ref[:, 0:1] * param_w_ref[0:1, :]
    for i in range(1, params_ref.shape[1]):
        from_params = from_params + params_ref[:, i : i + 1] * param_w_ref[i : i + 1, :]
    features = feature_sum.finish() / pooled
    hidden = jnp.tanh(mm(head_mask * features, wf) + from_params)
    logits = jnp.sum(hidden * out_w_ref[...], axis=1, keepdims=True)
    logits_ref[...] = logits
    dlogit = 1.0 / (1.0 + jnp.exp(-logits)) - labels_ref[...].astype(f32)
    dhidden = dlogit * out_w_ref[...] * (1.0 - hidden * hidden)
    dfeatures = jnp.sum(head_mask * mm(dhidden, wf, 1, 1), axis=0, keepdims=True)
    dpre1 = (dfeatures / pooled) * sig1
    d1_ref[...] = dpre1.reshape(nrows // 2, ncols, LANES)

    ex2 = exchange(2, d1_ref, False)
    ex2.start()

    grads = jnp.zeros((nch0, LANES), f32)
    for k in range(order):
        term = x1_ref[...] if k == 0 else t1_ref[k - 1]
        full = mask1 * mm(flat(term), dpre1, 0, 0)
        to_lane = onehot(ri % nch1 + k * nch1 == ci)
        grads = grads + mm(mm(at_ch0, full), to_lane)

    first, second = ex2.finish(flags_up, flags_down)
    dx1 = conv((d1_ref[...], first, second), w1, 1).reshape(nrows // 2, 1, ncols, LANES)
    sig0 = sig0_ref[...].reshape(nrows // 2, 2, ncols, LANES)
    d0_ref[...] = (dx1 * sig0).reshape(nrows, ncols, LANES)

    ex3 = exchange(3, d0_ref, True)
    ex3.start()
    dpre0 = flat(d0_ref[...])
    to_lane = onehot(ri % nch0 + order * nch1 == ci)
    for k in range(order):
        term = x0_ref[...] if k == 0 else t0_ref[k - 1]
        full = mask0 * mm(flat(term), dpre0, 0, 0)
        row, lane = iota((nch0, LANES), 0), iota((nch0, LANES), 1)
        to_row = onehot(lane % nbins + k * nbins == row)
        grads = grads + mm(mm(to_row, full), to_lane)

    low = low_slots.shape[0]
    tile_high, tile_low = lax.div(tile, low), lax.rem(tile, low)
    sums = [
        GroupSum(low_slots, sum_sems.at[1], tile_low, lambda j: (face, tile_high * low + j)),
        GroupSum(face_slots, sum_sems.at[2], face, lambda j: (j, tile)),
        GroupSum(high_slots, sum_sems.at[3], tile_high, lambda j: (face, j * low + tile_low)),
    ]
    sums[0].start(grads)
    first, second = ex3.finish(flags_up, flags_down)
    sums[1].start(sums[0].finish())
    pixels = float(nrows * faces * 2 * ncols * tiles)
    saliency = pixels * conv((d0_ref[...], first, second), w0, 1)
    sal_t_ref[...] = saliency.reshape(nrows, ncols, LANES)
    sums[2].start(sums[1].finish())
    wide = [p.astype(f32) for p in pairs]

    def store_row(r, _):
        row = sal_t_ref[r]
        total = mm(row, wide[0], 0, 0)[0:fields] + mm(row, wide[1], 0, 0)[HALF : HALF + fields]
        sal_ref[r] = total
        return 0

    lax.fori_loop(0, nrows, store_row, 0)
    grads = sums[2].finish()
    for k in range(order):
        grad_c_ref[k] = grads[:, k * nch1 : (k + 1) * nch1]
        start = order * nch1
        grad_f_ref[k] = grads[k * nbins : (k + 1) * nbins, start : start + nch0]


def on_device(faces, tiles, maps, params, labels, flip, fine_w, coarse_w, feature_w, param_w, out_w):
    nmaps, nbins, nrows, width = maps.shape
    ncols = width // 2
    low = 1
    while low * low < tiles:
        low *= 2
    vmem = pl.BlockSpec(memory_space=pltpu.VMEM)
    smem = pl.BlockSpec(memory_space=pltpu.SMEM)
    fine = (nrows, ncols, LANES)
    coarse = (nrows // 2, ncols, LANES)

    def buf(*shape):
        return pltpu.VMEM(shape, f32)

    logits, saliency, grad_f, grad_c = pl.pallas_call(
        functools.partial(kernel, faces, tiles),
        out_shape=(
            jax.ShapeDtypeStruct((nmaps, 1), f32),
            jax.ShapeDtypeStruct((nrows, nmaps * nbins, width), f32),
            jax.ShapeDtypeStruct(fine_w.shape, f32),
            jax.ShapeDtypeStruct(coarse_w.shape, f32),
        ),
        in_specs=[vmem, vmem, vmem, smem, vmem, vmem, vmem, vmem, vmem],
        out_specs=(vmem,) * 4,
        scratch_shapes=[
            buf(*fine),
            buf(2, *fine),
            buf(*fine),
            buf(*coarse),
            buf(2, *coarse),
            buf(*coarse),
            buf(*fine),
            buf(*fine),
            buf(2, 2, 2, ncols, LANES),
            buf(2, 2, 1, nrows, 1, LANES),
            buf(2, 2, 1, nrows, 1, LANES),
            buf(2, 2, 2, ncols, LANES),
            buf(2, 2, 2, nrows // 2, 1, LANES),
            buf(2, 2, 2, nrows // 2, 1, LANES),
            buf(4, 2, 2, 1, LANES),
            buf(4, 4, 2, 1, LANES),
            pltpu.SemaphoreType.DMA((4, 8)),
            pltpu.SemaphoreType.DMA((4, 8)),
            buf(faces * tiles, 1, LANES),
            buf(faces, fine_w.shape[2], LANES),
            buf(low, fine_w.shape[2], LANES),
            buf(tiles // low, fine_w.shape[2], LANES),
            pltpu.SemaphoreType.DMA((4, 2)),
        ],
        compiler_params=pltpu.CompilerParams(
            collective_id=0, has_side_effects=True, vmem_limit_bytes=48 * 1024 * 1024
        ),
    )(
        maps.reshape(nmaps * nbins, nrows, width).transpose(1, 0, 2),
        params,
        labels.reshape(nmaps, 1),
        flip,
        fine_w,
        coarse_w,
        feature_w,
        param_w,
        out_w.reshape(1, -1),
    )
    saliency = saliency.transpose(1, 0, 2).reshape(maps.shape)
    return logits.reshape(nmaps), saliency, grad_f, grad_c


def solution(mesh):
    in_specs = (P(None, None, "face", "tile"), P(), P(), P(), P(), P(), P(), P(), P())
    out_specs = (P(), P(None, None, "face", "tile"), P(), P())
    body = functools.partial(on_device, mesh.shape["face"], mesh.shape["tile"])
    return jax.shard_map(body, mesh=mesh, in_specs=in_specs, out_specs=out_specs, check_vma=False)
```

time: 218 us -> 54.4 us (0.25)
  blocking collectives: 77.8 us -> 0 us
  starting transfers between devices: 53.9 us -> 0 us
  Pallas kernels: 0 us -> 47.9 us
  waiting for transfers between devices: 36.5 us -> 0 us
  other arithmetic: 21.7 us -> 0.63 us
  local copies, waits for them, and re-layouts: 17 us -> 4.88 us
  matrix products: 8.29 us -> 0 us
    psum x2 -> x0, blocking collectives: 77.8 us -> none  [the longest x1 39 us: on_device(): grad_f, grad_c = lax.psum((grad_f, grad_c), ('face', 'tile'))]
    ppermute x32 -> x0, starting transfers between devices: 53.9 us -> none  [the longest x16 40.5 us: with_halo(): lax.ppermute(lax.slice_in_dim(block, 0, width, axis=dim), axis, backward)]
    pallas_call x0 -> x1, Pallas kernels: none -> 47.9 us  [on_device(): pl.pallas_call(functools.partial(kernel, faces, tiles), out_shape=(jax.Sh...]
    ppermute x32 -> x0, waiting for transfers between devices: 36.5 us -> none  [the longest x16 28.7 us: with_halo(): lax.ppermute(lax.slice_in_dim(block, block.shape[dim] - width, None, axis...]
    scatter x15 -> x0, other arithmetic: 10.7 us -> none  [the longest x8 6.22 us: stencil(): lower.at[..., -1, :]]
    dot_general x10 -> x0, matrix products: 8.29 us -> none  [the longest x1 1.71 us: on_device(): pre0 = jnp.einsum('kio,kbirc->borc', fine_weight, terms0, precision=exact)]
    reduce_sum x1 -> x0, other arithmetic: 5.64 us -> none  [on_device(): act0.reshape(nmaps, nchan, nrows // 2, 2, ncols // 2, 2).mean(axis=(3, 5))]
    broadcast_in_dim x1 -> x0, local copies, waits for them, and re-layouts: 4.04 us -> none  [on_device(): jnp.broadcast_to(dfield1[:, :, :, None, :, None], (nmaps, nchan, nrows //...]
  transfers between devices with their start and end apart: 32 -> 0, of which waited for: 21 -> 0; matrix products, arithmetic and copies ran while one was open for 8% -> 0% of each run, Pallas kernels for 0% -> 0%
where the time goes in v1:
time: 54.4 us; the launch traced here: 54.1 us
  Pallas kernels  47.9 us (88%)
  local copies, waits for them, and re-layouts  4.88 us (9%)
  between operations  0.71 us (1%)
  other arithmetic  0.63 us (1%)
    pallas_call x1, Pallas kernels, on_device(): pl.pallas_call(functools.partial(kernel, faces, tiles), out_shape=(jax.Sh...  47.9 us
    unnamed x21, local copies, waits for them, and re-layouts  4.78 us

profile of v1, /device:TPU:0, one launch (start us, length us, event | category | flops | bytes accessed | tf_op | source)
XLA Modules:
  0.0 54.1 jit_solution(8912389088471122373)
XLA Ops:
  0.6 0.0 copy-start.6
  0.6 0.7 %copy-done.6 = f32[4,2]{0,1:T(2,128)S(1)} copy-done((f32[4,2]{0,1:T(2,128)S(1)}, f32[4,2]{0,1:T(2,128)}, u32[]{:S(2)}) %copy-start.6) | copy-done | bytes 56
  1.3 0.0 copy-start.7
  1.3 0.1 copy.18.params_ref
  1.4 0.6 %copy-done.7 = s32[4]{0:T(128)S(1)} copy-done((s32[4]{0:T(128)S(1)}, s32[4]{0:T(128)}, u32[]{:S(2)}) %copy-start.7) | copy-done | bytes 40
  2.0 0.1 copy.19.labels_ref
  2.1 0.0 copy-start
  2.1 0.0 copy-start.1
  2.1 0.0 copy-start.2
  2.1 0.0 copy-start.4
  2.1 0.9 %copy.17 = bf16[4,4,16,128]{3,1,0,2:T(4,128)(2,1)S(1)} copy(bf16[4,4,16,128]{3,2,1,0:T(8,128)(2,1)} %param.9) | data formatting | bytes 131072 | tf_op args[0]
  3.0 0.0 copy-start.3
  3.0 0.0 copy-start.5
  3.0 0.0 copy-done
  3.0 0.0 copy-done.1
  3.0 0.0 copy-done.2
  3.0 0.0 copy-done.4
  3.1 0.6 %copy-done.3 = s32[2,16]{1,0:T(2,128)S(1)} copy-done((s32[2,16]{1,0:T(2,128)S(1)}, s32[2,16]{1,0:T(2,128)}, u32[]{:S(2)}) %copy-start.3) | copy-done | bytes 152
  3.7 0.0 copy-done.5
  3.7 47.9 %shard_map.120 = (f32[4,1]{1,0:T(4,128)S(1)}, f32[16,16,128]{2,1,0:T(8,128)S(1)}, f32[3,4,16]{2,1,0:T(4,128)S(1)}, f32[3,16,32]{2,1,0:T(8,128)S(1)}) custom-call(bf16[16,16,128]{2,1,0:T(8,128)(2,1)S(1)} %bitcast.8, f32[4,2]{1,0:T(4,128)S(1)} %copy.18.params_ref, s32[4,1]{1,0:T(4,128)S(1)} %copy.19.labels_ref, s32[2,16]{1,0:T(2,128)S(1)} %copy-done.3, ...), custom_call_target="tpu_custom_call" | custom-call | tf_op jit(solution)/shard_map/pallas_call | solution.py:424
  51.6 0.6 %reduce = f32[4]{0:T(128)} reduce(f32[4,1]{1,0:T(4,128)S(1)} %get-tuple-element.8, f32[]{:T(128)} %constant), dimensions={1}, to_apply=%get-tuple-element.8.reduce_sub_computation | reduce | bytes 36 | tf_op jit(solution)/shard_map/pallas_call | solution.py:424
  52.2 0.7 %copy.20 = f32[4,4,16,128]{3,2,1,0:T(8,128)} copy(f32[4,4,16,128]{3,1,0,2:T(4,128)S(1)} %bitcast.9) | data formatting | bytes 262144
  52.9 0.6 %copy.23 = f32[3,4,16]{2,1,0:T(4,128)} copy(f32[3,4,16]{2,1,0:T(4,128)S(1)} %get-tuple-element.26) | data formatting | bytes 1536
  53.5 0.6 %copy.24 = f32[3,16,32]{2,1,0:T(8,128)} copy(f32[3,16,32]{2,1,0:T(8,128)S(1)} %get-tuple-element.27) | data formatting | bytes 12288
Async XLA Ops:
  0.6 0.7 %copy-start.6 = (f32[4,2]{0,1:T(2,128)S(1)}, f32[4,2]{0,1:T(2,128)}, u32[]{:S(2)}) copy-start(f32[4,2]{0,1:T(2,128)} %param.10) | copy-start | bytes 100
  1.3 0.7 %copy-start.7 = (s32[4]{0:T(128)S(1)}, s32[4]{0:T(128)}, u32[]{:S(2)}) copy-start(s32[4]{0:T(128)} %param.11) | copy-start | bytes 52
  2.1 1.0 %copy-start = (f32[3,16,32]{2,1,0:T(8,128)S(1)}, f32[3,16,32]{2,1,0:T(8,128)}, u32[]{:S(2)}) copy-start(f32[3,16,32]{2,1,0:T(8,128)} %coarse_ref.1) | copy-start | bytes 18436
  2.1 1.0 %copy-start.1 = (f32[32,128]{1,0:T(8,128)S(1)}, f32[32,128]{1,0:T(8,128)}, u32[]{:S(2)}) copy-start(f32[32,128]{1,0:T(8,128)} %feature_ref.1) | copy-start | bytes 49156
  2.1 1.0 %copy-start.2 = (f32[3,4,16]{2,1,0:T(4,128)S(1)}, f32[3,4,16]{2,1,0:T(4,128)}, u32[]{:S(2)}) copy-start(f32[3,4,16]{2,1,0:T(4,128)} %fine_ref.1) | copy-start | bytes 2308
  2.1 1.0 %copy-start.4 = (f32[2,128]{1,0:T(2,128)S(1)}, f32[2,128]{1,0:T(2,128)}, u32[]{:S(2)}) copy-start(f32[2,128]{1,0:T(2,128)} %param_w_ref.1) | copy-start | bytes 3076
  3.0 0.7 %copy-start.3 = (s32[2,16]{1,0:T(2,128)S(1)}, s32[2,16]{1,0:T(2,128)}, u32[]{:S(2)}) copy-start(s32[2,16]{1,0:T(2,128)} %flip_ref.1) | copy-start | bytes 388
  3.0 0.7 %copy-start.5 = (f32[128]{0:T(128)S(1)}, f32[128]{0:T(128)}, u32[]{:S(2)}) copy-start(f32[128]{0:T(128)} %param.17) | copy-start | bytes 1540

commit v2 on v1

--- a/solution.py
+++ b/solution.py
@@ -8,6 +8,7 @@
 from jax.sharding import PartitionSpec as P
 
 f32 = jnp.float32
+bf16 = jnp.bfloat16
 exact = lax.Precision.HIGHEST
 MESH = pl.DeviceIdType.MESH
 LANES = 128
@@ -19,6 +20,18 @@
     return lax.dot_general(
         a, b, (((ca,), (cb,)), ((), ())), precision=precision, preferred_element_type=f32
     )
+
+
+def split(x):
+    high = x.astype(bf16)
+    return high, (x - high.astype(f32)).astype(bf16)
+
+
+def mm3(a, b, ca=1, cb=0):
+    (ah, al), (bh, bl) = a, b
+    left = jnp.concatenate([ah, al, ah], axis=ca)
+    right = jnp.concatenate([bh, bh, bl], axis=cb)
+    return mm(left, right, ca, cb, None)
 
 
 def iota(shape, dim):
@@ -62,10 +75,52 @@
     return -0.25 * (above + below + beside(x, left, right, fine))
 
 
+def lane_block(shape, size):
+    return (iota(shape, len(shape) - 1) % HALF) // size
+
+
+def pack_input(size, near, far):
+    pair = near + pltpu.roll(far, size, axis=1)
+    n = pair.shape[0] // 2
+    return pair[:n] + pltpu.roll(pair[n:], 2 * size, axis=1)
+
+
+def unpack_input(size, packed):
+    def block(i):
+        here = packed if i == 0 else pltpu.roll(packed, LANES - i * size, axis=1)
+        return jnp.where(lane_block(here.shape, size) == 0, here, 0.0)
+
+    near = jnp.concatenate([block(0), block(2)], axis=0)
+    far = jnp.concatenate([block(1), block(3)], axis=0)
+    return near, far
+
+
+def pack_pooled(near, far):
+    low = iota(near.shape, 1) < HALF
+    return jnp.where(low, near + swap(near), far + swap(far))
+
+
+def unpack_pooled(packed):
+    low = iota(packed.shape, 1) < HALF
+    return jnp.where(low, packed, 0.0), jnp.where(low, 0.0, packed)
+
+
+def pack_mixed(size, near, far):
+    return jnp.where(
+        lane_block(near.shape, size) == 3, pltpu.roll(far, size, axis=1), near
+    )
+
+
+def unpack_mixed(size, packed):
+    return packed, pltpu.roll(packed, LANES - size, axis=1)
+
+
 class Exchange:
-    def __init__(self, field, bufs, send_sem, recv_sem, place, fine):
+    def __init__(self, field, bufs, send_sem, recv_sem, place, fine, pack, unpack):
         self.field, self.place, self.fine = field, place, fine
-        self.row_recv, self.col_send, self.col_recv, self.end_send, self.end_recv = bufs
+        self.pack, self.unpack = pack, unpack
+        self.row_send, self.row_recv = bufs[:2]
+        self.col_send, self.col_recv, self.end_send, self.end_recv = bufs[2:]
         self.send_sem, self.recv_sem = send_sem, recv_sem
 
     def start(self):
@@ -86,32 +141,45 @@
             )
             copies[way].start()
 
-        send(UP, field.at[pl.ds(0, 2)], self.row_recv.at[1], (up, tile))
-        send(DOWN, field.at[pl.ds(nrows - 2, 2)], self.row_recv.at[0], (down, tile))
+        if self.pack is None:
+            send(UP, field.at[pl.ds(0, 2)], self.row_recv.at[1], (up, tile))
+            send(DOWN, field.at[pl.ds(nrows - 2, 2)], self.row_recv.at[0], (down, tile))
+        else:
+            self.row_send[0] = self.pack(field[0], field[1])
+            send(UP, self.row_send.at[0], self.row_recv.at[1], (up, tile))
+            self.row_send[1] = self.pack(field[nrows - 1], field[nrows - 2])
+            send(DOWN, self.row_send.at[1], self.row_recv.at[0], (down, tile))
+        for side, row in ((0, 0), (1, nrows - 1)):
+            self.end_send[side, 0] = field[row, 0:1, :]
+            self.end_send[side, 1] = field[row, ncols - 1 : ncols, :]
+        send(UL, self.end_send.at[0], self.end_recv.at[3], (up, left))
+        send(UR, self.end_send.at[0], self.end_recv.at[2], (up, right))
+        send(DL, self.end_send.at[1], self.end_recv.at[1], (down, left))
+        send(DR, self.end_send.at[1], self.end_recv.at[0], (down, right))
         width = self.col_send.shape[1]
         for w in range(width):
             self.col_send[0, w] = field[:, w : w + 1, :]
             self.col_send[1, w] = field[:, ncols - 1 - w : ncols - w, :]
-        for side, row in ((0, 0), (1, nrows - 1)):
-            self.end_send[side, 0] = field[row, 0:1, :]
-            self.end_send[side, 1] = field[row, ncols - 1 : ncols, :]
         send(LEFT, self.col_send.at[0], self.col_recv.at[1], (face, left))
         send(RIGHT, self.col_send.at[1], self.col_recv.at[0], (face, right))
-        send(UL, self.end_send.at[0], self.end_recv.at[3], (up, left))
-        send(UR, self.end_send.at[0], self.end_recv.at[2], (up, right))
-        send(DL, self.end_send.at[1], self.end_recv.at[1], (down, left))
-        send(DR, self.end_send.at[1], self.end_recv.at[0], (down, right))
         self.copies = copies
+
+    def rows(self, side):
+        got = self.row_recv[side]
+        if self.pack is None:
+            return (got[1], got[0]) if side == 0 else (got[0], got[1])
+        return self.unpack(got)
 
     def turn(self, x):
         return swap(x) if self.fine else x
 
     def outer(self, flags, rows, end_left, end_right):
         flag_left, flag, flag_right = flags
-        ncols = rows.shape[1]
-        mirror = onehot(iota((ncols, ncols), 0) + iota((ncols, ncols), 1) == ncols - 1)
-        pair = jnp.concatenate([rows[0], rows[1]], axis=1)
-        turned = mm(mirror, pair)
+        ncols = rows[0].shape[0]
+        at = (ncols, 2 * ncols)
+        mirror = onehot(iota(at, 0) + iota(at, 1) % ncols == ncols - 1).astype(bf16)
+        pair = jnp.concatenate(split(jnp.concatenate(rows, axis=1)), axis=0)
+        turned = mm(mirror, pair, 1, 0, None)
         rows = [
             pick(flag, self.turn(turned[:, LANES * i : LANES * (i + 1)]), rows[i]) for i in range(2)
         ]
@@ -121,15 +189,15 @@
         col_right = pick(flag_right, self.turn(end_right[1]), end_right[0])
         return rows, row_left, row_right, col_left, col_right
 
-    def finish(self, flags_up, flags_down):
+    def finish(self, flags_up, flags_down, mix=None):
         for copy in self.copies:
             copy.wait()
         fine = self.fine
         x = self.field[...]
         nrows, ncols, _ = x.shape
         ends = self.end_recv[...]
-        (u2, u1), ul, ur, lu, ru = self.outer(flags_up, self.row_recv[0], ends[0], ends[1])
-        (d1, d2), dl, dr, ld, rd = self.outer(flags_down, self.row_recv[1], ends[2], ends[3])
+        (u1, u2), ul, ur, lu, ru = self.outer(flags_up, self.rows(0), ends[0], ends[1])
+        (d1, d2), dl, dr, ld, rd = self.outer(flags_down, self.rows(1), ends[2], ends[3])
         lefts, rights = self.col_recv[0], self.col_recv[1]
         first = lap(x, u1, d1, lefts[0], rights[0], fine)
         first_u = -0.25 * (u2 + x[0] + beside(u1, ul, ur, fine))
@@ -148,8 +216,16 @@
 
         first_l = edge(lefts[0], lu, ld, along_l)
         first_r = edge(rights[0], ru, rd, along_r)
-        second = 2.0 * lap(first, first_u, first_d, first_l, first_r, fine) - x
-        return first, second
+        if mix is None:
+            return first, 2.0 * lap(first, first_u, first_d, first_l, first_r, fine) - x
+        return first, lap(
+            mix(x, first),
+            mix(u1, first_u),
+            mix(d1, first_d),
+            mix(lefts[0], first_l),
+            mix(rights[0], first_r),
+            fine,
+        )
 
 
 class GroupSum:
@@ -209,11 +285,16 @@
     t1_ref,
     d1_ref,
     d0_ref,
-    sal_t_ref,
-    fine_rows,
+    flat_ref,
+    input_rows_send,
+    input_rows_recv,
+    pooled_rows_send,
+    pooled_rows_recv,
+    mixed_rows_send,
+    mixed_rows_recv,
+    deep_rows_recv,
     fine_col_send,
     fine_col_recv,
-    coarse_rows,
     coarse_col_send,
     coarse_col_recv,
     end_send,
@@ -234,8 +315,8 @@
     nch1 = coarse_ref.shape[2]
     nmaps = params_ref.shape[0]
     order = fine_ref.shape[0]
-    nrows = maps_ref.shape[0]
-    ncols = maps_ref.shape[2] // 2
+    nrows = maps_ref.shape[2]
+    ncols = maps_ref.shape[3] // 2
     fields = nmaps * nbins
     pooled = float(nrows // 2 * ncols * devices)
 
@@ -255,33 +336,38 @@
 
     lax.fori_loop(1, devices, greet, 0)
 
-    col = iota((ncols, 2 * ncols), 1)
-    pairs = [
-        onehot(col == 2 * iota((ncols, 2 * ncols), 0) + p).astype(jnp.bfloat16) for p in range(2)
-    ]
-
-    zero = jnp.zeros((HALF - fields, 2 * ncols), jnp.bfloat16)
-
-    def load_row(r, _):
-        row = jnp.concatenate([maps_ref[r], zero], axis=0)
-        halves = [mm(pairs[p], row, 1, 1, None) for p in range(2)]
-        x0_ref[r] = jnp.concatenate(halves, axis=1)
-        return 0
-
-    lax.fori_loop(0, nrows, load_row, 0)
+    square = (LANES, LANES)
+    ri, ci = iota(square, 0), iota(square, 1)
+    even_first = onehot(ri == 2 * (ci % HALF) + ci // HALF).astype(bf16)
+    flat_ref[...] = mm(maps_ref[...].reshape(-1, LANES), even_first, 1, 0, None)
+    low_half = iota((fields, LANES), 1) < HALF
+    zero = jnp.zeros((HALF - fields, LANES), f32)
+
+    def row_of(r):
+        return flat_ref.at[pl.ds(r, fields, stride=nrows)]
+
+    for r in range(0, nrows, 2):
+        one, two = row_of(r)[...], row_of(r + 1)[...]
+        even = jnp.where(low_half, one, swap(two))
+        odd = jnp.where(low_half, swap(one), two)
+        both = jnp.concatenate([even, zero, odd, zero], axis=0)
+        x0_ref[pl.ds(r, 2)] = both.T.reshape(2, ncols, LANES)
+
     pl.semaphore_wait(barrier, devices - 1)
 
-    def exchange(i, field, fine):
-        rows, sends, recvs = (
-            (fine_rows, fine_col_send, fine_col_recv)
-            if fine
-            else (coarse_rows, coarse_col_send, coarse_col_recv)
-        )
-        slot = i // 2
-        bufs = (rows.at[slot], sends.at[slot], recvs.at[slot], end_send.at[i], end_recv.at[i])
-        return Exchange(field, bufs, halo_send.at[i], halo_recv.at[i], place, fine)
-
-    ex0 = exchange(0, x0_ref, True)
+    def exchange(i, field, rows, fine, pack, unpack):
+        cols = (fine_col_send, fine_col_recv) if fine else (coarse_col_send, coarse_col_recv)
+        bufs = rows + tuple(c.at[i // 2] for c in cols) + (end_send.at[i], end_recv.at[i])
+        return Exchange(field, bufs, halo_send.at[i], halo_recv.at[i], place, fine, pack, unpack)
+
+    ex0 = exchange(
+        0,
+        x0_ref,
+        (input_rows_send, input_rows_recv),
+        True,
+        functools.partial(pack_input, fields),
+        functools.partial(unpack_input, fields),
+    )
     ex0.start()
 
     below = lax.rem(face + 1, faces)
@@ -289,20 +375,34 @@
     flags_up = [jnp.where(flip_ref[face, s] == 1, 1.0, 0.0).astype(f32) for s in spots]
     flags_down = [jnp.where(flip_ref[below, s] == 1, 1.0, 0.0).astype(f32) for s in spots]
 
-    square = (LANES, LANES)
-    ri, ci = iota(square, 0), iota(square, 1)
-    mask0 = onehot(
-        (ri // HALF == ci // HALF)
-        & (ri % HALF < fields)
-        & ((ri % HALF) // nbins == (ci % HALF) // nch0)
-    )
+    at_bin = onehot(iota((LANES, nbins), 0) % nbins == iota((LANES, nbins), 1)).astype(bf16)
+    at_ch0 = onehot(iota((nch0, LANES), 1) % nch0 == iota((nch0, LANES), 0)).astype(bf16)
+    at_ch1 = onehot(iota((nch1, LANES), 1) % nch1 == iota((nch1, LANES), 0)).astype(bf16)
+
+    def spread(left, term, right, ca):
+        rows = mm(left, term, ca, 0, None)
+        return mm(rows.astype(bf16), right, 1, 0, None) if right is not None else rows
+
+    def fine_mask(k):
+        return onehot(
+            (ri // HALF == ci // HALF)
+            & ((ri % HALF) // fields == k)
+            & ((ri % fields) // nbins == (ci % HALF) // nch0)
+        )
+
+    mask0 = fine_mask(0)
     mask1 = onehot((ri % HALF) // nch0 == ci // nch1)
-    at_bin = onehot(iota((LANES, nbins), 0) % nbins == iota((LANES, nbins), 1))
-    at_ch0 = onehot(iota((nch0, LANES), 1) % nch0 == iota((nch0, LANES), 0))
-    at_ch1 = onehot(iota((nch1, LANES), 1) % nch1 == iota((nch1, LANES), 0))
-    w0 = [mask0 * mm(mm(at_bin, fine_ref[k]), at_ch0) for k in range(order)]
-    w1 = [mask1 * mm(mm(at_ch0, coarse_ref[k], 0, 0), at_ch1) for k in range(order)]
-    wf = mm(at_ch1, feature_ref[...], 0, 0)
+    w0, mixing = [], [0.0, 0.0]
+    for k in range(order):
+        terms = [spread(at_bin, t, at_ch0, 1) for t in split(fine_ref[k])]
+        w0.append([(mask0 * t).astype(bf16) for t in terms])
+        mixing = [m + fine_mask(k) * t for m, t in zip(mixing, terms)]
+    mixing = [m.astype(bf16) for m in mixing]
+    w1 = [
+        [(mask1 * spread(at_ch0, t, at_ch1, 0)).astype(bf16) for t in split(coarse_ref[k])]
+        for k in range(order)
+    ]
+    wf = [spread(at_ch1, t, None, 0).astype(bf16) for t in split(feature_ref[...])]
     head_mask = onehot(iota((nmaps, LANES), 0) == iota((nmaps, LANES), 1) // nch1)
 
     first, second = ex0.finish(flags_up, flags_down)
@@ -313,10 +413,11 @@
         return x.reshape(-1, LANES)
 
     def conv(terms, weights, cb):
-        total = mm(flat(terms[0]), weights[0], 1, cb)
-        for k in range(1, order):
-            total = total + mm(flat(terms[k]), weights[k], 1, cb)
-        return total
+        highs, lows = zip(*[split(flat(t)) for t in terms])
+        whighs, wlows = zip(*weights)
+        left = jnp.concatenate(highs + lows + highs, axis=1)
+        right = jnp.concatenate(whighs + whighs + wlows, axis=cb)
+        return mm(left, right, 1, cb, None)
 
     pre0 = conv((x0_ref[...], first, second), w0, 0)
     small = jnp.exp(-jnp.abs(pre0))
@@ -327,7 +428,9 @@
     act0 = act0.reshape(nrows // 2, 2, ncols, LANES)
     x1_ref[...] = 0.25 * (act0[:, 0] + act0[:, 1])
 
-    ex1 = exchange(1, x1_ref, False)
+    ex1 = exchange(
+        1, x1_ref, (pooled_rows_send, pooled_rows_recv), False, pack_pooled, unpack_pooled
+    )
     ex1.start()
     first, second = ex1.finish(flags_up, flags_down)
     t1_ref[0] = first
@@ -342,40 +445,61 @@
     for i in range(1, params_ref.shape[1]):
         from_params = from_params + params_ref[:, i : i + 1] * param_w_ref[i : i + 1, :]
     features = feature_sum.finish() / pooled
-    hidden = jnp.tanh(mm(head_mask * features, wf) + from_params)
+    hidden = jnp.tanh(mm3(split(head_mask * features), wf) + from_params)
     logits = jnp.sum(hidden * out_w_ref[...], axis=1, keepdims=True)
-    logits_ref[...] = logits
+    spot = iota((nmaps, nmaps), 0) == iota((nmaps, nmaps), 1)
+    logits_ref[...] = jnp.sum(jnp.where(spot, logits, 0.0), axis=0, keepdims=True)
     dlogit = 1.0 / (1.0 + jnp.exp(-logits)) - labels_ref[...].astype(f32)
     dhidden = dlogit * out_w_ref[...] * (1.0 - hidden * hidden)
-    dfeatures = jnp.sum(head_mask * mm(dhidden, wf, 1, 1), axis=0, keepdims=True)
+    dfeatures = jnp.sum(head_mask * mm3(split(dhidden), wf, 1, 1), axis=0, keepdims=True)
     dpre1 = (dfeatures / pooled) * sig1
     d1_ref[...] = dpre1.reshape(nrows // 2, ncols, LANES)
 
-    ex2 = exchange(2, d1_ref, False)
+    ex2 = exchange(2, d1_ref, (None, deep_rows_recv), False, None, None)
     ex2.start()
 
+    row, lane = iota((nch0, LANES), 0), iota((nch0, LANES), 1)
     grads = jnp.zeros((nch0, LANES), f32)
+    right = split(dpre1)
     for k in range(order):
         term = x1_ref[...] if k == 0 else t1_ref[k - 1]
-        full = mask1 * mm(flat(term), dpre1, 0, 0)
-        to_lane = onehot(ri % nch1 + k * nch1 == ci)
-        grads = grads + mm(mm(at_ch0, full), to_lane)
+        full = mask1 * mm3(split(flat(term)), right, 0, 0)
+        part = jnp.sum(full.reshape(-1, nch0, LANES), axis=0)
+        shift = LANES // 2
+        while shift >= nch1:
+            part = part + pltpu.roll(part, shift, axis=1)
+            shift //= 2
+        grads = jnp.where(lane // nch1 == k, part, grads)
 
     first, second = ex2.finish(flags_up, flags_down)
     dx1 = conv((d1_ref[...], first, second), w1, 1).reshape(nrows // 2, 1, ncols, LANES)
     sig0 = sig0_ref[...].reshape(nrows // 2, 2, ncols, LANES)
-    d0_ref[...] = (dx1 * sig0).reshape(nrows, ncols, LANES)
-
-    ex3 = exchange(3, d0_ref, True)
+    dpre0 = split(flat((dx1 * sig0).reshape(nrows, ncols, LANES)))
+
+    d0_ref[...] = mm3(dpre0, mixing, 1, 1).reshape(nrows, ncols, LANES)
+    ex3 = exchange(
+        3,
+        d0_ref,
+        (mixed_rows_send, mixed_rows_recv),
+        True,
+        functools.partial(pack_mixed, fields),
+        functools.partial(unpack_mixed, fields),
+    )
     ex3.start()
-    dpre0 = flat(d0_ref[...])
-    to_lane = onehot(ri % nch0 + order * nch1 == ci)
     for k in range(order):
         term = x0_ref[...] if k == 0 else t0_ref[k - 1]
-        full = mask0 * mm(flat(term), dpre0, 0, 0)
-        row, lane = iota((nch0, LANES), 0), iota((nch0, LANES), 1)
-        to_row = onehot(lane % nbins + k * nbins == row)
-        grads = grads + mm(mm(to_row, full), to_lane)
+        full = mask0 * mm3(split(flat(term)), dpre0, 0, 0)
+        part = full[0:fields] + full[HALF : HALF + fields]
+        shift = fields // 2
+        while shift >= nbins:
+            part = part + pltpu.roll(part, shift, axis=0)
+            shift //= 2
+        shift = LANES // 2
+        while shift >= nch0:
+            part = part + pltpu.roll(part, shift, axis=1)
+            shift //= 2
+        here = (row // nbins == k) & (lane // nch0 == order * nch1 // nch0)
+        grads = jnp.where(here, part, grads)
 
     low = low_slots.shape[0]
     tile_high, tile_low = lax.div(tile, low), lax.rem(tile, low)
@@ -385,21 +509,27 @@
         GroupSum(high_slots, sum_sems.at[3], tile_high, lambda j: (face, j * low + tile_low)),
     ]
     sums[0].start(grads)
-    first, second = ex3.finish(flags_up, flags_down)
+    def mix(x, first):
+        return x + 2.0 * pltpu.roll(first, LANES - fields, axis=first.ndim - 1)
+
+    _, outer = ex3.finish(flags_up, flags_down, mix)
     sums[1].start(sums[0].finish())
+    block = lane_block((nrows, ncols, LANES), fields)
+    mixed = d0_ref[...]
     pixels = float(nrows * faces * 2 * ncols * tiles)
-    saliency = pixels * conv((d0_ref[...], first, second), w0, 1)
-    sal_t_ref[...] = saliency.reshape(nrows, ncols, LANES)
+    parts = pixels * jnp.where(block == 0, mixed, jnp.where(block == 1, outer, -mixed))
+    for r in range(0, nrows, 2):
+        both = parts[r : r + 2].reshape(LANES, LANES).T
+        even, odd = [
+            both[h : h + fields] + both[h + fields : h + 2 * fields] + both[h + 2 * fields : h + 3 * fields]
+            for h in (0, HALF)
+        ]
+        row_of(r)[...] = jnp.where(low_half, even, swap(odd))
+        row_of(r + 1)[...] = jnp.where(low_half, swap(even), odd)
     sums[2].start(sums[1].finish())
-    wide = [p.astype(f32) for p in pairs]
-
-    def store_row(r, _):
-        row = sal_t_ref[r]
-        total = mm(row, wide[0], 0, 0)[0:fields] + mm(row, wide[1], 0, 0)[HALF : HALF + fields]
-        sal_ref[r] = total
-        return 0
-
-    lax.fori_loop(0, nrows, store_row, 0)
+    woven = jnp.concatenate(split(flat_ref[...]), axis=1)
+    twice = jnp.concatenate([even_first, even_first], axis=1)
+    sal_ref[...] = mm(woven, twice, 1, 1, None).reshape(sal_ref.shape)
     grads = sums[2].finish()
     for k in range(order):
         grad_c_ref[k] = grads[:, k * nch1 : (k + 1) * nch1]
@@ -424,8 +554,8 @@
     logits, saliency, grad_f, grad_c = pl.pallas_call(
         functools.partial(kernel, faces, tiles),
         out_shape=(
-            jax.ShapeDtypeStruct((nmaps, 1), f32),
-            jax.ShapeDtypeStruct((nrows, nmaps * nbins, width), f32),
+            jax.ShapeDtypeStruct((1, nmaps), f32),
+            jax.ShapeDtypeStruct(maps.shape, f32),
             jax.ShapeDtypeStruct(fine_w.shape, f32),
             jax.ShapeDtypeStruct(coarse_w.shape, f32),
         ),
@@ -439,11 +569,16 @@
             buf(2, *coarse),
             buf(*coarse),
             buf(*fine),
-            buf(*fine),
-            buf(2, 2, 2, ncols, LANES),
+            buf(nmaps * nbins * nrows, width),
+            buf(2, ncols // 2, LANES),
+            buf(2, ncols // 2, LANES),
+            buf(2, ncols, LANES),
+            buf(2, ncols, LANES),
+            buf(2, ncols, LANES),
+            buf(2, ncols, LANES),
+            buf(2, 2, ncols, LANES),
             buf(2, 2, 1, nrows, 1, LANES),
             buf(2, 2, 1, nrows, 1, LANES),
-            buf(2, 2, 2, ncols, LANES),
             buf(2, 2, 2, nrows // 2, 1, LANES),
             buf(2, 2, 2, nrows // 2, 1, LANES),
             buf(4, 2, 2, 1, LANES),
@@ -460,7 +595,7 @@
             collective_id=0, has_side_effects=True, vmem_limit_bytes=48 * 1024 * 1024
         ),
     )(
-        maps.reshape(nmaps * nbins, nrows, width).transpose(1, 0, 2),
+        maps,
         params,
         labels.reshape(nmaps, 1),
         flip,
@@ -470,7 +605,6 @@
         param_w,
         out_w.reshape(1, -1),
     )
-    saliency = saliency.transpose(1, 0, 2).reshape(maps.shape)
     return logits.reshape(nmaps), saliency, grad_f, grad_c
 
 

time: 54.4 us -> 48.2 us (0.89)
  Pallas kernels: 47.9 us -> 41 us
  local copies, waits for them, and re-layouts: 4.88 us -> 6.13 us
  other arithmetic: 0.63 us -> 0 us
    pallas_call x1, Pallas kernels: 47.9 us -> 41 us  [on_device(): pl.pallas_call(functools.partial(kernel, faces, tiles), out_shape=(jax.Sh...]
    unnamed x21, local copies, waits for them, and re-layouts: 4.78 us -> 6.04 us
    pallas_call x1 -> x0, other arithmetic: 0.63 us -> none  [on_device(): pl.pallas_call(functools.partial(kernel, faces, tiles), out_shape=(jax.Sh...]
where the time goes in v2:
time: 48.2 us; the launch traced here: 47.8 us
  Pallas kernels  41 us (85%)
  local copies, waits for them, and re-layouts  6.13 us (13%)
  between operations  0.67 us (1%)
    pallas_call x1, Pallas kernels, on_device(): pl.pallas_call(functools.partial(kernel, faces, tiles), out_shape=(jax.Sh...  41 us
    unnamed x21, local copies, waits for them, and re-layouts  6.04 us

profile of v2, /device:TPU:0, one launch (start us, length us, event | category | flops | bytes accessed | tf_op | source)
XLA Modules:
  0.0 47.8 jit_solution(11981196324509307204)
XLA Ops:
  0.6 0.0 copy-start.3
  0.6 0.0 copy-start.7
  0.7 0.8 %copy.13.params_ref = f32[4,2]{1,0:T(4,128)S(1)} copy(f32[4,2]{0,1:T(2,128)} %param.10) | data formatting | bytes 64 | tf_op args[1]
  1.4 0.0 copy-done.7
  1.4 0.0 copy-start.4
  1.4 0.0 copy-start.5
  1.4 0.0 copy-start.6
  1.4 0.1 copy.14.labels_ref
  1.5 0.0 copy-done.3
  1.5 0.6 %copy-done.4 = s32[2,16]{1,0:T(2,128)S(1)} copy-done((s32[2,16]{1,0:T(2,128)S(1)}, s32[2,16]{1,0:T(2,128)}, u32[]{:S(2)}) %copy-start.4) | copy-done | bytes 152
  2.1 0.0 copy-done.5
  2.1 0.0 copy-done.6
  2.1 0.0 copy-start
  2.1 0.8 %copy-done = bf16[4,4,16,128]{3,2,1,0:T(8,128)(2,1)S(1)} copy-done((bf16[4,4,16,128]{3,2,1,0:T(8,128)(2,1)S(1)}, bf16[4,4,16,128]{3,2,1,0:T(8,128)(2,1)}, u32[]{:S(2)}) %copy-start) | copy-done | bytes 65560
  3.0 0.0 copy-start.1
  3.0 0.7 %copy-done.1 = f32[3,16,32]{2,1,0:T(8,128)S(1)} copy-done((f32[3,16,32]{2,1,0:T(8,128)S(1)}, f32[3,16,32]{2,1,0:T(8,128)}, u32[]{:S(2)}) %copy-start.1) | copy-done | bytes 6168
  3.7 0.0 copy-start.2
  3.7 0.7 %copy-done.2 = f32[32,128]{1,0:T(8,128)S(1)} copy-done((f32[32,128]{1,0:T(8,128)S(1)}, f32[32,128]{1,0:T(8,128)}, u32[]{:S(2)}) %copy-start.2) | copy-done | bytes 16408
  4.4 41.0 %shard_map.120 = (f32[1,4]{1,0:T(1,128)S(1)}, f32[4,4,16,128]{3,2,1,0:T(8,128)S(1)}, f32[3,4,16]{2,1,0:T(4,128)S(1)}, f32[3,16,32]{2,1,0:T(8,128)S(1)}) custom-call(bf16[4,4,16,128]{3,2,1,0:T(8,128)(2,1)S(1)} %copy-done, f32[4,2]{1,0:T(4,128)S(1)} %copy.13.params_ref, s32[4,1]{1,0:T(4,128)S(1)} %copy.14.labels_ref, s32[2,16]{1,0:T(2,128)S(1)} %copy-done.4, ...), custom_call_target="tpu_custom_call" | custom-call | tf_op jit(solution)/shard_map/pallas_call | solution.py:554
  45.5 0.5 %copy.19 = f32[4]{0:T(128)} copy(f32[4]{0:T(128)S(1)} %bitcast.4) | data formatting | bytes 32
  46.0 0.7 %copy.20 = f32[4,4,16,128]{3,2,1,0:T(8,128)} copy(f32[4,4,16,128]{3,2,1,0:T(8,128)S(1)} %get-tuple-element.17) | data formatting | bytes 262144
  46.6 0.6 %copy.21 = f32[3,4,16]{2,1,0:T(4,128)} copy(f32[3,4,16]{2,1,0:T(4,128)S(1)} %get-tuple-element.18) | data formatting | bytes 1536
  47.2 0.6 %copy.22 = f32[3,16,32]{2,1,0:T(8,128)} copy(f32[3,16,32]{2,1,0:T(8,128)S(1)} %get-tuple-element.19) | data formatting | bytes 12288
Async XLA Ops:
  0.6 0.9 %copy-start.3 = (f32[3,4,16]{2,1,0:T(4,128)S(1)}, f32[3,4,16]{2,1,0:T(4,128)}, u32[]{:S(2)}) copy-start(f32[3,4,16]{2,1,0:T(4,128)} %fine_ref.1) | copy-start | bytes 2308
  0.6 0.8 %copy-start.7 = (s32[4]{0:T(128)S(1)}, s32[4]{0:T(128)}, u32[]{:S(2)}) copy-start(s32[4]{0:T(128)} %param.11) | copy-start | bytes 52
  1.4 0.7 %copy-start.4 = (s32[2,16]{1,0:T(2,128)S(1)}, s32[2,16]{1,0:T(2,128)}, u32[]{:S(2)}) copy-start(s32[2,16]{1,0:T(2,128)} %flip_ref.1) | copy-start | bytes 388
  1.4 0.7 %copy-start.5 = (f32[2,128]{1,0:T(2,128)S(1)}, f32[2,128]{1,0:T(2,128)}, u32[]{:S(2)}) copy-start(f32[2,128]{1,0:T(2,128)} %param_w_ref.1) | copy-start | bytes 3076
  1.4 0.7 %copy-start.6 = (f32[128]{0:T(128)S(1)}, f32[128]{0:T(128)}, u32[]{:S(2)}) copy-start(f32[128]{0:T(128)} %param.17) | copy-start | bytes 1540
  2.1 0.8 %copy-start = (bf16[4,4,16,128]{3,2,1,0:T(8,128)(2,1)S(1)}, bf16[4,4,16,128]{3,2,1,0:T(8,128)(2,1)}, u32[]{:S(2)}) copy-start(bf16[4,4,16,128]{3,2,1,0:T(8,128)(2,1)} %maps_ref.1) | copy-start | bytes 196612
  3.0 0.7 %copy-start.1 = (f32[3,16,32]{2,1,0:T(8,128)S(1)}, f32[3,16,32]{2,1,0:T(8,128)}, u32[]{:S(2)}) copy-start(f32[3,16,32]{2,1,0:T(8,128)} %coarse_ref.1) | copy-start | bytes 18436
  3.7 0.7 %copy-start.2 = (f32[32,128]{1,0:T(8,128)S(1)}, f32[32,128]{1,0:T(8,128)}, u32[]{:S(2)}) copy-start(f32[32,128]{1,0:T(8,128)} %feature_ref.1) | copy-start | bytes 49156

commit v3 on v2

--- a/solution.py
+++ b/solution.py
@@ -229,42 +229,102 @@
 
 
 class GroupSum:
-    def __init__(self, slots, sems, me, device_of):
-        self.slots, self.sems, self.me, self.device_of = slots, sems, me, device_of
+    def __init__(self, slots, sems, me, visit):
+        self.slots, self.sems, self.me, self.visit = slots, sems, me, visit
         self.count = slots.shape[0]
 
     def start(self, value):
-        me, count = self.me, self.count
-        self.slots[me] = value
-
-        def step(k, _):
+        mine = self.slots.at[self.me]
+        mine[...] = value
+
+        def send(device):
             pltpu.make_async_remote_copy(
-                src_ref=self.slots.at[me],
-                dst_ref=self.slots.at[me],
+                src_ref=mine,
+                dst_ref=mine,
                 send_sem=self.sems.at[0],
                 recv_sem=self.sems.at[1],
-                device_id=self.device_of(lax.rem(me + k, count)),
+                device_id=device,
                 device_id_type=MESH,
             ).start()
-            return 0
-
-        lax.fori_loop(1, count, step, 0)
+
+        self.visit(send)
 
     def finish(self):
         others = self.slots.at[pl.ds(0, self.count - 1)]
         pltpu.make_async_copy(others, others, self.sems.at[1]).wait()
         pltpu.make_async_copy(others, others, self.sems.at[0]).wait()
-        total = self.slots[0]
-        if self.count <= 8:
-            for i in range(1, self.count):
-                total = total + self.slots[i]
-            return total
         return jnp.sum(self.slots[...], axis=0)
+
+
+def ring(me, count, device_of):
+    def visit(act):
+        for k in range(1, count):
+            act(device_of(lax.rem(me + k, count)))
+
+    return visit
+
+
+def everyone(face, tile, faces, tiles):
+    def row(act, f, first):
+        where = face if isinstance(f, int) and f == 0 else lax.rem(face + f, faces)
+
+        def step(t, _):
+            act((where, lax.rem(tile + t, tiles)))
+            return 0
+
+        if tiles <= 16:
+            for t in range(first, tiles):
+                step(t, 0)
+        else:
+            lax.fori_loop(first, tiles, step, 0)
+
+    def visit(act):
+        row(act, 0, 1)
+
+        def other(f, _):
+            row(act, f, 0)
+            return 0
+
+        if faces <= 2:
+            for f in range(1, faces):
+                other(f, 0)
+        else:
+            lax.fori_loop(1, faces, other, 0)
+
+    return visit
+
+
+def write_kernel(*refs):
+    count = len(refs) // 2
+    sems = refs[-1]
+    copies = [
+        pltpu.make_async_copy(refs[i], refs[count + i], sems.at[i]) for i in range(count)
+    ]
+    for copy in copies:
+        copy.start()
+    for copy in copies:
+        copy.wait()
 
 
 def kernel(
     faces,
     tiles,
+    *refs,
+):
+    inputs, outputs, held = refs[:9], refs[9:13], refs[13:22]
+    input_sems, work = refs[22], refs[23:]
+    loads = [
+        pltpu.make_async_copy(inputs[i], held[i], input_sems.at[i]) for i in range(len(inputs))
+    ]
+    for load in loads:
+        load.start()
+    run(faces, tiles, loads, *held, *outputs, *work)
+
+
+def run(
+    faces,
+    tiles,
+    loads,
     maps_ref,
     params_ref,
     labels_ref,
@@ -313,32 +373,25 @@
     linear = face * tiles + tile
     nbins, nch0 = fine_ref.shape[1:]
     nch1 = coarse_ref.shape[2]
-    nmaps = params_ref.shape[0]
+    nmaps = params_ref.shape[1]
     order = fine_ref.shape[0]
     nrows = maps_ref.shape[2]
     ncols = maps_ref.shape[3] // 2
     fields = nmaps * nbins
     pooled = float(nrows // 2 * ncols * devices)
 
-    def device_of(i):
-        return (lax.div(i, tiles), lax.rem(i, tiles))
-
+    to_everyone = everyone(face, tile, faces, tiles)
     barrier = pltpu.get_barrier_semaphore()
 
-    def greet(k, _):
-        pl.semaphore_signal(
-            barrier,
-            inc=1,
-            device_id=device_of(lax.rem(linear + k, devices)),
-            device_id_type=MESH,
-        )
-        return 0
-
-    lax.fori_loop(1, devices, greet, 0)
+    def greet(device):
+        pl.semaphore_signal(barrier, inc=1, device_id=device, device_id_type=MESH)
+
+    to_everyone(greet)
 
     square = (LANES, LANES)
     ri, ci = iota(square, 0), iota(square, 1)
     even_first = onehot(ri == 2 * (ci % HALF) + ci // HALF).astype(bf16)
+    loads[0].wait()
     flat_ref[...] = mm(maps_ref[...].reshape(-1, LANES), even_first, 1, 0, None)
     low_half = iota((fields, LANES), 1) < HALF
     zero = jnp.zeros((HALF - fields, LANES), f32)
@@ -369,6 +422,8 @@
         functools.partial(unpack_input, fields),
     )
     ex0.start()
+    for load in loads[1:]:
+        load.wait()
 
     below = lax.rem(face + 1, faces)
     spots = (lax.rem(tile + tiles - 1, tiles), tile, lax.rem(tile + 1, tiles))
@@ -404,6 +459,11 @@
     ]
     wf = [spread(at_ch1, t, None, 0).astype(bf16) for t in split(feature_ref[...])]
     head_mask = onehot(iota((nmaps, LANES), 0) == iota((nmaps, LANES), 1) // nch1)
+    from_params = mm(params_ref[...], param_w_ref[...], 0, 0)
+    spot = iota((nmaps, nmaps), 0) == iota((nmaps, nmaps), 1)
+    labels = jnp.sum(
+        jnp.where(spot, labels_ref[...].astype(f32), 0.0), axis=1, keepdims=True
+    )
 
     first, second = ex0.finish(flags_up, flags_down)
     t0_ref[0] = first
@@ -438,41 +498,34 @@
     pre1 = conv((x1_ref[...], first, second), w1, 0)
     small = jnp.exp(-jnp.abs(pre1))
     act1 = jnp.maximum(pre1, 0.0) + jnp.log1p(small)
-    feature_sum = GroupSum(feature_slots, sum_sems.at[0], linear, device_of)
+    feature_sum = GroupSum(feature_slots, sum_sems.at[0], linear, to_everyone)
     feature_sum.start(jnp.sum(act1, axis=0, keepdims=True))
+
     sig1 = jnp.where(pre1 >= 0, 1.0, small) / (1.0 + small)
-    from_params = params_ref[:, 0:1] * param_w_ref[0:1, :]
-    for i in range(1, params_ref.shape[1]):
-        from_params = from_params + params_ref[:, i : i + 1] * param_w_ref[i : i + 1, :]
+    d1_ref[...] = sig1.reshape(nrows // 2, ncols, LANES)
+    ex2 = exchange(2, d1_ref, (None, deep_rows_recv), False, None, None)
+    ex2.start()
+
+    row, lane = iota((nch0, LANES), 0), iota((nch0, LANES), 1)
+    unscaled = []
+    right = split(sig1)
+    for k in range(order):
+        term = x1_ref[...] if k == 0 else t1_ref[k - 1]
+        full = mask1 * mm3(split(flat(term)), right, 0, 0)
+        unscaled.append(jnp.sum(full.reshape(-1, nch0, LANES), axis=0))
+
     features = feature_sum.finish() / pooled
     hidden = jnp.tanh(mm3(split(head_mask * features), wf) + from_params)
     logits = jnp.sum(hidden * out_w_ref[...], axis=1, keepdims=True)
-    spot = iota((nmaps, nmaps), 0) == iota((nmaps, nmaps), 1)
     logits_ref[...] = jnp.sum(jnp.where(spot, logits, 0.0), axis=0, keepdims=True)
-    dlogit = 1.0 / (1.0 + jnp.exp(-logits)) - labels_ref[...].astype(f32)
+    dlogit = 1.0 / (1.0 + jnp.exp(-logits)) - labels
     dhidden = dlogit * out_w_ref[...] * (1.0 - hidden * hidden)
     dfeatures = jnp.sum(head_mask * mm3(split(dhidden), wf, 1, 1), axis=0, keepdims=True)
-    dpre1 = (dfeatures / pooled) * sig1
-    d1_ref[...] = dpre1.reshape(nrows // 2, ncols, LANES)
-
-    ex2 = exchange(2, d1_ref, (None, deep_rows_recv), False, None, None)
-    ex2.start()
-
-    row, lane = iota((nch0, LANES), 0), iota((nch0, LANES), 1)
-    grads = jnp.zeros((nch0, LANES), f32)
-    right = split(dpre1)
-    for k in range(order):
-        term = x1_ref[...] if k == 0 else t1_ref[k - 1]
-        full = mask1 * mm3(split(flat(term)), right, 0, 0)
-        part = jnp.sum(full.reshape(-1, nch0, LANES), axis=0)
-        shift = LANES // 2
-        while shift >= nch1:
-            part = part + pltpu.roll(part, shift, axis=1)
-            shift //= 2
-        grads = jnp.where(lane // nch1 == k, part, grads)
+    scale = dfeatures / pooled
+    scaled = [split(scale * (h.astype(f32) + l.astype(f32))) for h, l in w1]
 
     first, second = ex2.finish(flags_up, flags_down)
-    dx1 = conv((d1_ref[...], first, second), w1, 1).reshape(nrows // 2, 1, ncols, LANES)
+    dx1 = conv((d1_ref[...], first, second), scaled, 1).reshape(nrows // 2, 1, ncols, LANES)
     sig0 = sig0_ref[...].reshape(nrows // 2, 2, ncols, LANES)
     dpre0 = split(flat((dx1 * sig0).reshape(nrows, ncols, LANES)))
 
@@ -486,6 +539,14 @@
         functools.partial(unpack_mixed, fields),
     )
     ex3.start()
+    grads = jnp.zeros((nch0, LANES), f32)
+    for k in range(order):
+        part = scale * unscaled[k]
+        shift = LANES // 2
+        while shift >= nch1:
+            part = part + pltpu.roll(part, shift, axis=1)
+            shift //= 2
+        grads = jnp.where(lane // nch1 == k, part, grads)
     for k in range(order):
         term = x0_ref[...] if k == 0 else t0_ref[k - 1]
         full = mask0 * mm3(split(flat(term)), dpre0, 0, 0)
@@ -503,10 +564,14 @@
 
     low = low_slots.shape[0]
     tile_high, tile_low = lax.div(tile, low), lax.rem(tile, low)
+    groups = (
+        (low_slots, tile_low, lambda j: (face, tile_high * low + j)),
+        (face_slots, face, lambda j: (j, tile)),
+        (high_slots, tile_high, lambda j: (face, j * low + tile_low)),
+    )
     sums = [
-        GroupSum(low_slots, sum_sems.at[1], tile_low, lambda j: (face, tile_high * low + j)),
-        GroupSum(face_slots, sum_sems.at[2], face, lambda j: (j, tile)),
-        GroupSum(high_slots, sum_sems.at[3], tile_high, lambda j: (face, j * low + tile_low)),
+        GroupSum(slots, sum_sems.at[1 + i], me, ring(me, slots.shape[0], device_of))
+        for i, (slots, me, device_of) in enumerate(groups)
     ]
     sums[0].start(grads)
     def mix(x, first):
@@ -544,14 +609,27 @@
     while low * low < tiles:
         low *= 2
     vmem = pl.BlockSpec(memory_space=pltpu.VMEM)
-    smem = pl.BlockSpec(memory_space=pltpu.SMEM)
     fine = (nrows, ncols, LANES)
     coarse = (nrows // 2, ncols, LANES)
 
     def buf(*shape):
         return pltpu.VMEM(shape, f32)
 
-    logits, saliency, grad_f, grad_c = pl.pallas_call(
+    operands = (
+        maps,
+        params.T,
+        labels.reshape(1, nmaps),
+        flip,
+        fine_w,
+        coarse_w,
+        feature_w,
+        param_w,
+        out_w.reshape(1, -1),
+    )
+    held = [pltpu.VMEM(x.shape, x.dtype) for x in operands]
+    held[3] = pltpu.SMEM(flip.shape, flip.dtype)
+    anywhere = pl.BlockSpec(memory_space=pl.ANY)
+    results = pl.pallas_call(
         functools.partial(kernel, faces, tiles),
         out_shape=(
             jax.ShapeDtypeStruct((1, nmaps), f32),
@@ -559,9 +637,11 @@
             jax.ShapeDtypeStruct(fine_w.shape, f32),
             jax.ShapeDtypeStruct(coarse_w.shape, f32),
         ),
-        in_specs=[vmem, vmem, vmem, smem, vmem, vmem, vmem, vmem, vmem],
+        in_specs=[anywhere] * len(operands),
         out_specs=(vmem,) * 4,
         scratch_shapes=[
+            *held,
+            pltpu.SemaphoreType.DMA((len(operands),)),
             buf(*fine),
             buf(2, *fine),
             buf(*fine),
@@ -592,19 +672,17 @@
             pltpu.SemaphoreType.DMA((4, 2)),
         ],
         compiler_params=pltpu.CompilerParams(
-            collective_id=0, has_side_effects=True, vmem_limit_bytes=48 * 1024 * 1024
+            collective_id=0, has_side_effects=True, vmem_limit_bytes=60 * 1024 * 1024
         ),
-    )(
-        maps,
-        params,
-        labels.reshape(nmaps, 1),
-        flip,
-        fine_w,
-        coarse_w,
-        feature_w,
-        param_w,
-        out_w.reshape(1, -1),
-    )
+    )(*operands)
+    logits, saliency, grad_f, grad_c = pl.pallas_call(
+        write_kernel,
+        out_shape=tuple(jax.ShapeDtypeStruct(x.shape, x.dtype) for x in results),
+        in_specs=[anywhere] * len(results),
+        out_specs=(anywhere,) * len(results),
+        scratch_shapes=[pltpu.SemaphoreType.DMA((len(results),))],
+        compiler_params=pltpu.CompilerParams(vmem_limit_bytes=60 * 1024 * 1024),
+    )(*results)
     return logits.reshape(nmaps), saliency, grad_f, grad_c
 
 

time: 48.2 us -> 42.9 us (0.89)
  local copies, waits for them, and re-layouts: 6.13 us -> 0 us
  Pallas kernels: 41 us -> 42.1 us
    pallas_call x0 -> x1, Pallas kernels: none -> 6.06 us  [on_device(): pl.pallas_call(write_kernel, out_shape=tuple((jax.ShapeDtypeStruct(x.shap...]
    unnamed x21 -> x0, local copies, waits for them, and re-layouts: 6.04 us -> none
    pallas_call x1, Pallas kernels: 41 us -> 36 us  [on_device(): pl.pallas_call(functools.partial(kernel, faces, tiles), out_shape=(jax.Sh...]
where the time goes in v3:
time: 42.9 us; the launch traced here: 42.7 us
  Pallas kernels  42.1 us (98%)
  between operations  0.64 us (1%)
    pallas_call x1, Pallas kernels, on_device(): pl.pallas_call(functools.partial(kernel, faces, tiles), out_shape=(jax.Sh...  36 us
    pallas_call x1, Pallas kernels, on_device(): pl.pallas_call(write_kernel, out_shape=tuple((jax.ShapeDtypeStruct(x.shap...  6.06 us

profile of v3, /device:TPU:0, one launch (start us, length us, event | category | flops | bytes accessed | tf_op | source)
XLA Modules:
  0.0 42.7 jit_solution(4635762479379384696)
XLA Ops:
  0.6 36.0 %shard_map.120 = (f32[1,4]{1,0:T(1,128)}, f32[4,4,16,128]{3,2,1,0:T(8,128)}, f32[3,4,16]{2,1,0:T(4,128)}, f32[3,16,32]{2,1,0:T(8,128)}) custom-call(bf16[4,4,16,128]{3,2,1,0:T(8,128)(2,1)} %refs_0_.1, f32[2,4]{1,0:T(2,128)} %bitcast.4, s32[1,4]{1,0:T(1,128)} %bitcast.5, s32[2,16]{1,0:T(2,128)} %refs_3_.1, f32[3,4,16]{2,1,0:T(4,128)} %refs_4_.1, ...), custom_call_target="tpu_custom_call" | custom-call | tf_op jit(solution)/shard_map/pallas_call | solution.py:632
  36.7 6.1 %shard_map.121 = (f32[1,4]{1,0:T(1,128)}, f32[4,4,16,128]{3,2,1,0:T(8,128)}, f32[3,4,16]{2,1,0:T(4,128)}, f32[3,16,32]{2,1,0:T(8,128)}) custom-call(f32[1,4]{1,0:T(1,128)} %get-tuple-element.12.refs_0_, f32[4,4,16,128]{3,2,1,0:T(8,128)} %get-tuple-element.13.refs_1_, f32[3,4,16]{2,1,0:T(4,128)} %get-tuple-element.14.refs_2_, ...), custom_call_target="tpu_custom_call" | custom-call | tf_op jit(solution)/shard_map/pallas_call | solution.py:678

commit v4 on v3

--- a/solution.py
+++ b/solution.py
@@ -69,10 +69,10 @@
     return s + jnp.where(even, from_left(s, swap(left)), from_right(s, swap(right)))
 
 
-def lap(x, up, down, left, right, fine):
-    above = jnp.concatenate([up[None], x[:-1]], axis=0)
-    below = jnp.concatenate([x[1:], down[None]], axis=0)
-    return -0.25 * (above + below + beside(x, left, right, fine))
+def lap_row(ref, r, up, down, left, right, fine):
+    above = up if r == 0 else ref[r - 1]
+    below = down if r == ref.shape[0] - 1 else ref[r + 1]
+    return -0.25 * (above + below + beside(ref[r], left, right, fine))
 
 
 def lane_block(shape, size):
@@ -189,43 +189,41 @@
         col_right = pick(flag_right, self.turn(end_right[1]), end_right[0])
         return rows, row_left, row_right, col_left, col_right
 
-    def finish(self, flags_up, flags_down, mix=None):
+    def finish(self, flags_up, flags_down, first_ref, emit, mix=None):
         for copy in self.copies:
             copy.wait()
-        fine = self.fine
-        x = self.field[...]
+        fine, x = self.fine, self.field
         nrows, ncols, _ = x.shape
         ends = self.end_recv[...]
         (u1, u2), ul, ur, lu, ru = self.outer(flags_up, self.rows(0), ends[0], ends[1])
         (d1, d2), dl, dr, ld, rd = self.outer(flags_down, self.rows(1), ends[2], ends[3])
         lefts, rights = self.col_recv[0], self.col_recv[1]
-        first = lap(x, u1, d1, lefts[0], rights[0], fine)
-        first_u = -0.25 * (u2 + x[0] + beside(u1, ul, ur, fine))
-        first_d = -0.25 * (d2 + x[nrows - 1] + beside(d1, dl, dr, fine))
+
+        def through(x, first):
+            return first if mix is None else mix(x, first)
+
+        for r in range(nrows):
+            first = lap_row(x, r, u1, d1, lefts[0, r], rights[0, r], fine)
+            first_ref[r] = through(x[r], first)
+        first_u = through(u1, -0.25 * (u2 + x[0] + beside(u1, ul, ur, fine)))
+        first_d = through(d1, -0.25 * (d2 + x[nrows - 1] + beside(d1, dl, dr, fine)))
         if fine:
-            along_l = swap(lefts[0]) + swap(self.field[:, 0:1, :])
-            along_r = swap(rights[0]) + swap(self.field[:, ncols - 1 : ncols, :])
+            along_l = swap(lefts[0]) + swap(x[:, 0:1, :])
+            along_r = swap(rights[0]) + swap(x[:, ncols - 1 : ncols, :])
         else:
-            along_l = lefts[1] + self.field[:, 0:1, :]
-            along_r = rights[1] + self.field[:, ncols - 1 : ncols, :]
+            along_l = lefts[1] + x[:, 0:1, :]
+            along_r = rights[1] + x[:, ncols - 1 : ncols, :]
 
         def edge(col, over, under, along):
             above = jnp.concatenate([over[None], col[:-1]], axis=0)
             below = jnp.concatenate([col[1:], under[None]], axis=0)
-            return -0.25 * (above + below + along)
+            return through(col, -0.25 * (above + below + along))
 
         first_l = edge(lefts[0], lu, ld, along_l)
         first_r = edge(rights[0], ru, rd, along_r)
-        if mix is None:
-            return first, 2.0 * lap(first, first_u, first_d, first_l, first_r, fine) - x
-        return first, lap(
-            mix(x, first),
-            mix(u1, first_u),
-            mix(d1, first_d),
-            mix(lefts[0], first_l),
-            mix(rights[0], first_r),
-            fine,
-        )
+        for r in range(nrows):
+            second = lap_row(first_ref, r, first_u, first_d, first_l[r], first_r[r], fine)
+            emit(r, x[r], first_ref[r], second)
 
 
 class GroupSum:
@@ -295,15 +293,17 @@
 
 
 def write_kernel(*refs):
-    count = len(refs) // 2
-    sems = refs[-1]
-    copies = [
-        pltpu.make_async_copy(refs[i], refs[count + i], sems.at[i]) for i in range(count)
-    ]
-    for copy in copies:
-        copy.start()
-    for copy in copies:
-        copy.wait()
+    count = len(refs) // 3
+    sources, targets, held, sems = refs[:count], refs[count : 2 * count], refs[2 * count : -1], refs[-1]
+    loads = [pltpu.make_async_copy(sources[i], held[i], sems.at[0, i]) for i in range(count)]
+    stores = [pltpu.make_async_copy(held[i], targets[i], sems.at[1, i]) for i in range(count)]
+    for load in loads:
+        load.start()
+    for load, store in zip(loads, stores):
+        load.wait()
+        store.start()
+    for store in stores:
+        store.wait()
 
 
 def kernel(
@@ -311,20 +311,26 @@
     tiles,
     *refs,
 ):
-    inputs, outputs, held = refs[:9], refs[9:13], refs[13:22]
-    input_sems, work = refs[22], refs[23:]
+    inputs, outputs, held, made = refs[:9], refs[9:13], refs[13:22], refs[22:26]
+    input_sems, output_sems, work = refs[26], refs[27], refs[28:]
     loads = [
         pltpu.make_async_copy(inputs[i], held[i], input_sems.at[i]) for i in range(len(inputs))
     ]
     for load in loads:
         load.start()
-    run(faces, tiles, loads, *held, *outputs, *work)
+    stores = [
+        pltpu.make_async_copy(made[i], outputs[i], output_sems.at[i]) for i in range(len(outputs))
+    ]
+    run(faces, tiles, loads, stores, *held, *made, *work)
+    for store in stores:
+        store.wait()
 
 
 def run(
     faces,
     tiles,
     loads,
+    stores,
     maps_ref,
     params_ref,
     labels_ref,
@@ -339,12 +345,17 @@
     grad_f_ref,
     grad_c_ref,
     x0_ref,
-    t0_ref,
+    first0_ref,
+    split0_ref,
+    pre0_ref,
     sig0_ref,
     x1_ref,
-    t1_ref,
+    first1_ref,
+    split1_ref,
     d1_ref,
+    split_d1_ref,
     d0_ref,
+    split_d0_ref,
     flat_ref,
     input_rows_send,
     input_rows_recv,
@@ -445,13 +456,12 @@
             & ((ri % fields) // nbins == (ci % HALF) // nch0)
         )
 
-    mask0 = fine_mask(0)
+    mask0 = [fine_mask(k) for k in range(order)]
     mask1 = onehot((ri % HALF) // nch0 == ci // nch1)
-    w0, mixing = [], [0.0, 0.0]
+    mixing = [0.0, 0.0]
     for k in range(order):
         terms = [spread(at_bin, t, at_ch0, 1) for t in split(fine_ref[k])]
-        w0.append([(mask0 * t).astype(bf16) for t in terms])
-        mixing = [m + fine_mask(k) * t for m, t in zip(mixing, terms)]
+        mixing = [m + mask0[k] * t for m, t in zip(mixing, terms)]
     mixing = [m.astype(bf16) for m in mixing]
     w1 = [
         [(mask1 * spread(at_ch0, t, at_ch1, 0)).astype(bf16) for t in split(coarse_ref[k])]
@@ -465,71 +475,96 @@
         jnp.where(spot, labels_ref[...].astype(f32), 0.0), axis=1, keepdims=True
     )
 
-    first, second = ex0.finish(flags_up, flags_down)
-    t0_ref[0] = first
-    t0_ref[1] = second
-
-    def flat(x):
-        return x.reshape(-1, LANES)
-
-    def conv(terms, weights, cb):
-        highs, lows = zip(*[split(flat(t)) for t in terms])
-        whighs, wlows = zip(*weights)
-        left = jnp.concatenate(highs + lows + highs, axis=1)
-        right = jnp.concatenate(whighs + whighs + wlows, axis=cb)
-        return mm(left, right, 1, cb, None)
-
-    pre0 = conv((x0_ref[...], first, second), w0, 0)
-    small = jnp.exp(-jnp.abs(pre0))
-    act0 = jnp.maximum(pre0, 0.0) + jnp.log1p(small)
-    sig0_ref[...] = (0.25 * jnp.where(pre0 >= 0, 1.0, small) / (1.0 + small)).reshape(
-        nrows, ncols, LANES
-    )
-    act0 = act0.reshape(nrows // 2, 2, ncols, LANES)
-    x1_ref[...] = 0.25 * (act0[:, 0] + act0[:, 1])
+    def beside_lows(weights, axis):
+        highs, lows = [jnp.concatenate(w, axis=axis) for w in zip(*weights)]
+        return jnp.concatenate(
+            [
+                jnp.concatenate([highs, highs], axis=axis),
+                jnp.concatenate([lows, jnp.zeros_like(lows)], axis=axis),
+            ],
+            axis=1 - axis,
+        )
+
+    def folded(x):
+        return x[:, :LANES] + x[:, LANES:]
+
+    def put(ref, r, places, x):
+        for place, part in zip(places, split(x)):
+            ref[r * ncols : (r + 1) * ncols, place * LANES : (place + 1) * LANES] = part
+
+    def soft(v):
+        small = jnp.exp(-jnp.abs(v))
+        sig = jnp.where(v >= 0, 1.0, small) / (1.0 + small)
+        return jnp.maximum(v, 0.0) + jnp.log1p(small), sig
+
+    mix_forward, mix_back = beside_lows([mixing], 0), beside_lows([mixing], 1)
+
+    def emit_fine(r, x, first, outer):
+        second = 2.0 * outer - x
+        terms = x + pltpu.roll(first, fields, axis=1) + pltpu.roll(second, 2 * fields, axis=1)
+        put(split0_ref, r, (0, 1), terms)
+
+    ex0.finish(flags_up, flags_down, first0_ref, emit_fine)
+    pre0_ref[...] = folded(mm(split0_ref[...], mix_forward, 1, 0, None)).reshape(pre0_ref.shape)
+    for r in range(0, nrows, 2):
+        acts = []
+        for q in (r, r + 1):
+            act, sig = soft(pre0_ref[q])
+            sig0_ref[q] = 0.25 * sig
+            acts.append(act)
+        x1_ref[r // 2] = 0.25 * (acts[0] + acts[1])
 
     ex1 = exchange(
         1, x1_ref, (pooled_rows_send, pooled_rows_recv), False, pack_pooled, unpack_pooled
     )
     ex1.start()
-    first, second = ex1.finish(flags_up, flags_down)
-    t1_ref[0] = first
-    t1_ref[1] = second
-    pre1 = conv((x1_ref[...], first, second), w1, 0)
-    small = jnp.exp(-jnp.abs(pre1))
-    act1 = jnp.maximum(pre1, 0.0) + jnp.log1p(small)
+    coarse_forward = beside_lows(w1, 0)
+
+    def emit_coarse(r, x, first, outer):
+        for k, term in enumerate((x, first, 2.0 * outer - x)):
+            put(split1_ref, r, (k, order + k), term)
+
+    ex1.finish(flags_up, flags_down, first1_ref, emit_coarse)
+    pre1 = folded(mm(split1_ref[...], coarse_forward, 1, 0, None))
+    act_sum = jnp.zeros((ncols, LANES), f32)
+    for r in range(nrows // 2):
+        act, sig = soft(pre1[r * ncols : (r + 1) * ncols])
+        act_sum = act_sum + act
+        d1_ref[r] = sig
     feature_sum = GroupSum(feature_slots, sum_sems.at[0], linear, to_everyone)
-    feature_sum.start(jnp.sum(act1, axis=0, keepdims=True))
-
-    sig1 = jnp.where(pre1 >= 0, 1.0, small) / (1.0 + small)
-    d1_ref[...] = sig1.reshape(nrows // 2, ncols, LANES)
+    feature_sum.start(jnp.sum(act_sum, axis=0, keepdims=True))
+
     ex2 = exchange(2, d1_ref, (None, deep_rows_recv), False, None, None)
     ex2.start()
 
     row, lane = iota((nch0, LANES), 0), iota((nch0, LANES), 1)
+    for r in range(nrows // 2):
+        put(split_d1_ref, r, (0, 1), d1_ref[r])
+    products = mm(split1_ref[...], split_d1_ref[...], 0, 0, None)
     unscaled = []
-    right = split(sig1)
     for k in range(order):
-        term = x1_ref[...] if k == 0 else t1_ref[k - 1]
-        full = mask1 * mm3(split(flat(term)), right, 0, 0)
-        unscaled.append(jnp.sum(full.reshape(-1, nch0, LANES), axis=0))
+        full = folded(products[k * LANES : (k + 1) * LANES])
+        full = full + products[(order + k) * LANES : (order + k + 1) * LANES, :LANES]
+        unscaled.append(jnp.sum((mask1 * full).reshape(-1, nch0, LANES), axis=0))
 
     features = feature_sum.finish() / pooled
     hidden = jnp.tanh(mm3(split(head_mask * features), wf) + from_params)
     logits = jnp.sum(hidden * out_w_ref[...], axis=1, keepdims=True)
     logits_ref[...] = jnp.sum(jnp.where(spot, logits, 0.0), axis=0, keepdims=True)
+    stores[0].start()
     dlogit = 1.0 / (1.0 + jnp.exp(-logits)) - labels
     dhidden = dlogit * out_w_ref[...] * (1.0 - hidden * hidden)
     dfeatures = jnp.sum(head_mask * mm3(split(dhidden), wf, 1, 1), axis=0, keepdims=True)
     scale = dfeatures / pooled
     scaled = [split(scale * (h.astype(f32) + l.astype(f32))) for h, l in w1]
 
-    first, second = ex2.finish(flags_up, flags_down)
-    dx1 = conv((d1_ref[...], first, second), scaled, 1).reshape(nrows // 2, 1, ncols, LANES)
-    sig0 = sig0_ref[...].reshape(nrows // 2, 2, ncols, LANES)
-    dpre0 = split(flat((dx1 * sig0).reshape(nrows, ncols, LANES)))
-
-    d0_ref[...] = mm3(dpre0, mixing, 1, 1).reshape(nrows, ncols, LANES)
+    coarse_back = beside_lows(scaled, 1)
+    ex2.finish(flags_up, flags_down, first1_ref, emit_coarse)
+    dx1 = folded(mm(split1_ref[...], coarse_back, 1, 1, None))
+    for r in range(nrows):
+        put(split_d0_ref, r, (0, 1), dx1[r // 2 * ncols : (r // 2 + 1) * ncols] * sig0_ref[r])
+
+    d0_ref[...] = folded(mm(split_d0_ref[...], mix_back, 1, 1, None)).reshape(d0_ref.shape)
     ex3 = exchange(
         3,
         d0_ref,
@@ -547,10 +582,12 @@
             part = part + pltpu.roll(part, shift, axis=1)
             shift //= 2
         grads = jnp.where(lane // nch1 == k, part, grads)
+    products = mm(split0_ref[...], split_d0_ref[...], 0, 0, None)
+    products = folded(products[:LANES]) + products[LANES:, :LANES]
     for k in range(order):
-        term = x0_ref[...] if k == 0 else t0_ref[k - 1]
-        full = mask0 * mm3(split(flat(term)), dpre0, 0, 0)
-        part = full[0:fields] + full[HALF : HALF + fields]
+        full = mask0[k] * products
+        start = k * fields
+        part = full[start : start + fields] + full[HALF + start : HALF + start + fields]
         shift = fields // 2
         while shift >= nbins:
             part = part + pltpu.roll(part, shift, axis=0)
@@ -577,14 +614,16 @@
     def mix(x, first):
         return x + 2.0 * pltpu.roll(first, LANES - fields, axis=first.ndim - 1)
 
-    _, outer = ex3.finish(flags_up, flags_down, mix)
+    block = lane_block((ncols, LANES), fields)
+    pixels = float(nrows * faces * 2 * ncols * tiles)
+
+    def emit_back(r, x, first, outer):
+        sig0_ref[r] = pixels * jnp.where(block == 0, x, jnp.where(block == 1, outer, -x))
+
+    ex3.finish(flags_up, flags_down, first0_ref, emit_back, mix)
     sums[1].start(sums[0].finish())
-    block = lane_block((nrows, ncols, LANES), fields)
-    mixed = d0_ref[...]
-    pixels = float(nrows * faces * 2 * ncols * tiles)
-    parts = pixels * jnp.where(block == 0, mixed, jnp.where(block == 1, outer, -mixed))
     for r in range(0, nrows, 2):
-        both = parts[r : r + 2].reshape(LANES, LANES).T
+        both = sig0_ref[pl.ds(r, 2)].reshape(LANES, LANES).T
         even, odd = [
             both[h : h + fields] + both[h + fields : h + 2 * fields] + both[h + 2 * fields : h + 3 * fields]
             for h in (0, HALF)
@@ -595,11 +634,14 @@
     woven = jnp.concatenate(split(flat_ref[...]), axis=1)
     twice = jnp.concatenate([even_first, even_first], axis=1)
     sal_ref[...] = mm(woven, twice, 1, 1, None).reshape(sal_ref.shape)
+    stores[1].start()
     grads = sums[2].finish()
     for k in range(order):
         grad_c_ref[k] = grads[:, k * nch1 : (k + 1) * nch1]
         start = order * nch1
         grad_f_ref[k] = grads[k * nbins : (k + 1) * nbins, start : start + nch0]
+    stores[2].start()
+    stores[3].start()
 
 
 def on_device(faces, tiles, maps, params, labels, flip, fine_w, coarse_w, feature_w, param_w, out_w):
@@ -608,7 +650,6 @@
     low = 1
     while low * low < tiles:
         low *= 2
-    vmem = pl.BlockSpec(memory_space=pltpu.VMEM)
     fine = (nrows, ncols, LANES)
     coarse = (nrows // 2, ncols, LANES)
 
@@ -629,26 +670,29 @@
     held = [pltpu.VMEM(x.shape, x.dtype) for x in operands]
     held[3] = pltpu.SMEM(flip.shape, flip.dtype)
     anywhere = pl.BlockSpec(memory_space=pl.ANY)
+    shapes = ((1, nmaps), maps.shape, fine_w.shape, coarse_w.shape)
     results = pl.pallas_call(
         functools.partial(kernel, faces, tiles),
-        out_shape=(
-            jax.ShapeDtypeStruct((1, nmaps), f32),
-            jax.ShapeDtypeStruct(maps.shape, f32),
-            jax.ShapeDtypeStruct(fine_w.shape, f32),
-            jax.ShapeDtypeStruct(coarse_w.shape, f32),
-        ),
+        out_shape=tuple(jax.ShapeDtypeStruct(shape, f32) for shape in shapes),
         in_specs=[anywhere] * len(operands),
-        out_specs=(vmem,) * 4,
+        out_specs=(anywhere,) * 4,
         scratch_shapes=[
             *held,
+            *[buf(*shape) for shape in shapes],
             pltpu.SemaphoreType.DMA((len(operands),)),
+            pltpu.SemaphoreType.DMA((len(shapes),)),
             buf(*fine),
-            buf(2, *fine),
+            buf(*fine),
+            pltpu.VMEM((nrows * ncols, 2 * LANES), bf16),
+            buf(*fine),
             buf(*fine),
             buf(*coarse),
-            buf(2, *coarse),
             buf(*coarse),
+            pltpu.VMEM((nrows // 2 * ncols, 2 * fine_w.shape[0] * LANES), bf16),
+            buf(*coarse),
+            pltpu.VMEM((nrows // 2 * ncols, 2 * LANES), bf16),
             buf(*fine),
+            pltpu.VMEM((nrows * ncols, 2 * LANES), bf16),
             buf(nmaps * nbins * nrows, width),
             buf(2, ncols // 2, LANES),
             buf(2, ncols // 2, LANES),
@@ -680,7 +724,10 @@
         out_shape=tuple(jax.ShapeDtypeStruct(x.shape, x.dtype) for x in results),
         in_specs=[anywhere] * len(results),
         out_specs=(anywhere,) * len(results),
-        scratch_shapes=[pltpu.SemaphoreType.DMA((len(results),))],
+        scratch_shapes=[
+            *[pltpu.VMEM(x.shape, x.dtype) for x in results],
+            pltpu.SemaphoreType.DMA((2, len(results))),
+        ],
         compiler_params=pltpu.CompilerParams(vmem_limit_bytes=60 * 1024 * 1024),
     )(*results)
     return logits.reshape(nmaps), saliency, grad_f, grad_c

time: 42.9 us -> 38.4 us (0.90)
  Pallas kernels: 42.1 us -> 37.6 us
    pallas_call x1, Pallas kernels: 6.06 us -> 1.64 us  [on_device(): pl.pallas_call(write_kernel, out_shape=tuple((jax.ShapeDtypeStruct(x.shap...]
where the time goes in v4:
time: 38.4 us; the launch traced here: 38.2 us
  Pallas kernels  37.6 us (98%)
  between operations  0.64 us (2%)
    pallas_call x1, Pallas kernels, on_device(): pl.pallas_call(functools.partial(kernel, faces, tiles), out_shape=tuple((...  35.9 us
    pallas_call x1, Pallas kernels, on_device(): pl.pallas_call(write_kernel, out_shape=tuple((jax.ShapeDtypeStruct(x.shap...  1.64 us

profile of v4, /device:TPU:0, one launch (start us, length us, event | category | flops | bytes accessed | tf_op | source)
XLA Modules:
  0.0 38.2 jit_solution(14282680918865260011)
XLA Ops:
  0.6 35.9 %shard_map.120 = (f32[1,4]{1,0:T(1,128)}, f32[4,4,16,128]{3,2,1,0:T(8,128)}, f32[3,4,16]{2,1,0:T(4,128)}, f32[3,16,32]{2,1,0:T(8,128)}) custom-call(bf16[4,4,16,128]{3,2,1,0:T(8,128)(2,1)} %refs_0_.1, f32[2,4]{1,0:T(2,128)} %bitcast.4, s32[1,4]{1,0:T(1,128)} %bitcast.5, s32[2,16]{1,0:T(2,128)} %refs_3_.1, f32[3,4,16]{2,1,0:T(4,128)} %refs_4_.1, ...), custom_call_target="tpu_custom_call" | custom-call | tf_op jit(solution)/shard_map/pallas_call | solution.py:674
  36.6 1.6 %shard_map.121 = (f32[1,4]{1,0:T(1,128)}, f32[4,4,16,128]{3,2,1,0:T(8,128)}, f32[3,4,16]{2,1,0:T(4,128)}, f32[3,16,32]{2,1,0:T(8,128)}) custom-call(f32[1,4]{1,0:T(1,128)} %get-tuple-element.12.refs_0_, f32[4,4,16,128]{3,2,1,0:T(8,128)} %get-tuple-element.13.refs_1_, f32[3,4,16]{2,1,0:T(4,128)} %get-tuple-element.14.refs_2_, ...), custom_call_target="tpu_custom_call" | custom-call | tf_op jit(solution)/shard_map/pallas_call | solution.py:722

commit v5 on v4

--- a/solution.py
+++ b/solution.py
@@ -256,8 +256,15 @@
 
 def ring(me, count, device_of):
     def visit(act):
-        for k in range(1, count):
+        def step(k, _):
             act(device_of(lax.rem(me + k, count)))
+            return 0
+
+        if count <= 8:
+            for k in range(1, count):
+                step(k, 0)
+        else:
+            lax.fori_loop(1, count, step, 0)
 
     return visit
 
@@ -373,8 +380,7 @@
     halo_send,
     halo_recv,
     feature_slots,
-    face_slots,
-    low_slots,
+    near_slots,
     high_slots,
     sum_sems,
 ):
@@ -441,33 +447,28 @@
     flags_up = [jnp.where(flip_ref[face, s] == 1, 1.0, 0.0).astype(f32) for s in spots]
     flags_down = [jnp.where(flip_ref[below, s] == 1, 1.0, 0.0).astype(f32) for s in spots]
 
-    at_bin = onehot(iota((LANES, nbins), 0) % nbins == iota((LANES, nbins), 1)).astype(bf16)
     at_ch0 = onehot(iota((nch0, LANES), 1) % nch0 == iota((nch0, LANES), 0)).astype(bf16)
     at_ch1 = onehot(iota((nch1, LANES), 1) % nch1 == iota((nch1, LANES), 0)).astype(bf16)
 
-    def spread(left, term, right, ca):
-        rows = mm(left, term, ca, 0, None)
-        return mm(rows.astype(bf16), right, 1, 0, None) if right is not None else rows
-
-    def fine_mask(k):
-        return onehot(
-            (ri // HALF == ci // HALF)
-            & ((ri % HALF) // fields == k)
-            & ((ri % fields) // nbins == (ci % HALF) // nch0)
-        )
-
-    mask0 = [fine_mask(k) for k in range(order)]
-    mask1 = onehot((ri % HALF) // nch0 == ci // nch1)
-    mixing = [0.0, 0.0]
-    for k in range(order):
-        terms = [spread(at_bin, t, at_ch0, 1) for t in split(fine_ref[k])]
-        mixing = [m + mask0[k] * t for m, t in zip(mixing, terms)]
-    mixing = [m.astype(bf16) for m in mixing]
-    w1 = [
-        [(mask1 * spread(at_ch0, t, at_ch1, 0)).astype(bf16) for t in split(coarse_ref[k])]
-        for k in range(order)
-    ]
-    wf = [spread(at_ch1, t, None, 0).astype(bf16) for t in split(feature_ref[...])]
+    def spread(left, terms, right, ca):
+        width = terms[0].shape[1]
+        rows = mm(left, jnp.concatenate(terms, axis=1), ca, 0, None).astype(bf16)
+        rows = [rows[:, i * width : (i + 1) * width] for i in range(len(terms))]
+        if right is None:
+            return rows
+        full = mm(jnp.concatenate(rows, axis=0), right, 1, 0, None)
+        return [full[i * LANES : (i + 1) * LANES] for i in range(len(terms))]
+
+    mask0 = onehot(
+        (ri // HALF == ci // HALF)
+        & ((ri % HALF) // fields < order)
+        & ((ri % fields) // nbins == (ci % HALF) // nch0)
+    )
+    rf, cf = iota((LANES, order * nbins), 0), iota((LANES, order * nbins), 1)
+    at_term = onehot(((rf % HALF) // fields == cf // nbins) & (rf % nbins == cf % nbins))
+    fine_w = jnp.concatenate([fine_ref[k] for k in range(order)], axis=0)
+    mixing = spread(at_term.astype(bf16), split(fine_w), at_ch0, 1)
+    mixing = [(mask0 * m).astype(bf16) for m in mixing]
     head_mask = onehot(iota((nmaps, LANES), 0) == iota((nmaps, LANES), 1) // nch1)
     from_params = mm(params_ref[...], param_w_ref[...], 0, 0)
     spot = iota((nmaps, nmaps), 0) == iota((nmaps, nmaps), 1)
@@ -518,6 +519,11 @@
         1, x1_ref, (pooled_rows_send, pooled_rows_recv), False, pack_pooled, unpack_pooled
     )
     ex1.start()
+    mask1 = onehot((ri % HALF) // nch0 == ci // nch1)
+    terms = [t for k in range(order) for t in split(coarse_ref[k])]
+    terms = [(mask1 * t).astype(bf16) for t in spread(at_ch0, terms, at_ch1, 0)]
+    w1 = [terms[2 * k : 2 * k + 2] for k in range(order)]
+    wf = spread(at_ch1, split(feature_ref[...]), None, 0)
     coarse_forward = beside_lows(w1, 0)
 
     def emit_coarse(r, x, first, outer):
@@ -583,9 +589,8 @@
             shift //= 2
         grads = jnp.where(lane // nch1 == k, part, grads)
     products = mm(split0_ref[...], split_d0_ref[...], 0, 0, None)
-    products = folded(products[:LANES]) + products[LANES:, :LANES]
+    full = mask0 * (folded(products[:LANES]) + products[LANES:, :LANES])
     for k in range(order):
-        full = mask0[k] * products
         start = k * fields
         part = full[start : start + fields] + full[HALF + start : HALF + start + fields]
         shift = fields // 2
@@ -599,11 +604,15 @@
         here = (row // nbins == k) & (lane // nch0 == order * nch1 // nch0)
         grads = jnp.where(here, part, grads)
 
-    low = low_slots.shape[0]
+    low = tiles // high_slots.shape[0]
     tile_high, tile_low = lax.div(tile, low), lax.rem(tile, low)
+    my_near = face * low + tile_low
+
+    def near_device(j):
+        return lax.div(j, low), tile_high * low + lax.rem(j, low)
+
     groups = (
-        (low_slots, tile_low, lambda j: (face, tile_high * low + j)),
-        (face_slots, face, lambda j: (j, tile)),
+        (near_slots, my_near, near_device),
         (high_slots, tile_high, lambda j: (face, j * low + tile_low)),
     )
     sums = [
@@ -620,8 +629,8 @@
     def emit_back(r, x, first, outer):
         sig0_ref[r] = pixels * jnp.where(block == 0, x, jnp.where(block == 1, outer, -x))
 
+    sums[1].start(sums[0].finish())
     ex3.finish(flags_up, flags_down, first0_ref, emit_back, mix)
-    sums[1].start(sums[0].finish())
     for r in range(0, nrows, 2):
         both = sig0_ref[pl.ds(r, 2)].reshape(LANES, LANES).T
         even, odd = [
@@ -630,12 +639,11 @@
         ]
         row_of(r)[...] = jnp.where(low_half, even, swap(odd))
         row_of(r + 1)[...] = jnp.where(low_half, swap(even), odd)
-    sums[2].start(sums[1].finish())
     woven = jnp.concatenate(split(flat_ref[...]), axis=1)
     twice = jnp.concatenate([even_first, even_first], axis=1)
     sal_ref[...] = mm(woven, twice, 1, 1, None).reshape(sal_ref.shape)
     stores[1].start()
-    grads = sums[2].finish()
+    grads = sums[1].finish()
     for k in range(order):
         grad_c_ref[k] = grads[:, k * nch1 : (k + 1) * nch1]
         start = order * nch1
@@ -710,8 +718,7 @@
             pltpu.SemaphoreType.DMA((4, 8)),
             pltpu.SemaphoreType.DMA((4, 8)),
             buf(faces * tiles, 1, LANES),
-            buf(faces, fine_w.shape[2], LANES),
-            buf(low, fine_w.shape[2], LANES),
+            buf(faces * low, fine_w.shape[2], LANES),
             buf(tiles // low, fine_w.shape[2], LANES),
             pltpu.SemaphoreType.DMA((4, 2)),
         ],

time: 38.4 us -> 35.2 us (0.917)
  Pallas kernels: 37.6 us -> 34.4 us
    pallas_call x1, Pallas kernels: 35.9 us -> 32.8 us  [on_device(): pl.pallas_call(functools.partial(kernel, faces, tiles), out_shape=tuple((...]
where the time goes in v5:
time: 35.2 us; the launch traced here: 35.1 us
  Pallas kernels  34.4 us (98%)
  between operations  0.64 us (2%)
    pallas_call x1, Pallas kernels, on_device(): pl.pallas_call(functools.partial(kernel, faces, tiles), out_shape=tuple((...  32.8 us
    pallas_call x1, Pallas kernels, on_device(): pl.pallas_call(write_kernel, out_shape=tuple((jax.ShapeDtypeStruct(x.shap...  1.64 us

profile of v5, /device:TPU:0, one launch (start us, length us, event | category | flops | bytes accessed | tf_op | source)
XLA Modules:
  0.0 35.1 jit_solution(8590821176986769898)
XLA Ops:
  0.6 32.8 %shard_map.120 = (f32[1,4]{1,0:T(1,128)}, f32[4,4,16,128]{3,2,1,0:T(8,128)}, f32[3,4,16]{2,1,0:T(4,128)}, f32[3,16,32]{2,1,0:T(8,128)}) custom-call(bf16[4,4,16,128]{3,2,1,0:T(8,128)(2,1)} %refs_0_.1, f32[2,4]{1,0:T(2,128)} %bitcast.4, s32[1,4]{1,0:T(1,128)} %bitcast.5, s32[2,16]{1,0:T(2,128)} %refs_3_.1, f32[3,4,16]{2,1,0:T(4,128)} %refs_4_.1, ...), custom_call_target="tpu_custom_call" | custom-call | tf_op jit(solution)/shard_map/pallas_call | solution.py:682
  33.4 1.6 %shard_map.121 = (f32[1,4]{1,0:T(1,128)}, f32[4,4,16,128]{3,2,1,0:T(8,128)}, f32[3,4,16]{2,1,0:T(4,128)}, f32[3,16,32]{2,1,0:T(8,128)}) custom-call(f32[1,4]{1,0:T(1,128)} %get-tuple-element.12.refs_0_, f32[4,4,16,128]{3,2,1,0:T(8,128)} %get-tuple-element.13.refs_1_, f32[3,4,16]{2,1,0:T(4,128)} %get-tuple-element.14.refs_2_, ...), custom_call_target="tpu_custom_call" | custom-call | tf_op jit(solution)/shard_map/pallas_call | solution.py:729

commit v6 on v5

--- a/solution.py
+++ b/solution.py
@@ -265,36 +265,6 @@
                 step(k, 0)
         else:
             lax.fori_loop(1, count, step, 0)
-
-    return visit
-
-
-def everyone(face, tile, faces, tiles):
-    def row(act, f, first):
-        where = face if isinstance(f, int) and f == 0 else lax.rem(face + f, faces)
-
-        def step(t, _):
-            act((where, lax.rem(tile + t, tiles)))
-            return 0
-
-        if tiles <= 16:
-            for t in range(first, tiles):
-                step(t, 0)
-        else:
-            lax.fori_loop(first, tiles, step, 0)
-
-    def visit(act):
-        row(act, 0, 1)
-
-        def other(f, _):
-            row(act, f, 0)
-            return 0
-
-        if faces <= 2:
-            for f in range(1, faces):
-                other(f, 0)
-        else:
-            lax.fori_loop(1, faces, other, 0)
 
     return visit
 
@@ -379,7 +349,8 @@
     end_recv,
     halo_send,
     halo_recv,
-    feature_slots,
+    feature_near,
+    feature_high,
     near_slots,
     high_slots,
     sum_sems,
@@ -387,7 +358,6 @@
     face, tile = lax.axis_index("face"), lax.axis_index("tile")
     place = (face, tile, faces, tiles)
     devices = faces * tiles
-    linear = face * tiles + tile
     nbins, nch0 = fine_ref.shape[1:]
     nch1 = coarse_ref.shape[2]
     nmaps = params_ref.shape[1]
@@ -397,13 +367,39 @@
     fields = nmaps * nbins
     pooled = float(nrows // 2 * ncols * devices)
 
-    to_everyone = everyone(face, tile, faces, tiles)
+    low = tiles // high_slots.shape[0]
+    tile_high, tile_low = lax.div(tile, low), lax.rem(tile, low)
+    my_near = face * low + tile_low
+
+    def near_device(j):
+        return lax.div(j, low), tile_high * low + lax.rem(j, low)
+
+    def high_device(j):
+        return face, j * low + tile_low
+
+    visit_near = ring(my_near, near_slots.shape[0], near_device)
+    visit_high = ring(tile_high, high_slots.shape[0], high_device)
+
+    def group_sums(near, high, i):
+        return [
+            GroupSum(near, sum_sems.at[i], my_near, visit_near),
+            GroupSum(high, sum_sems.at[i + 1], tile_high, visit_high),
+        ]
+
     barrier = pltpu.get_barrier_semaphore()
 
     def greet(device):
         pl.semaphore_signal(barrier, inc=1, device_id=device, device_id_type=MESH)
 
-    to_everyone(greet)
+    up, down = lax.rem(face + faces - 1, faces), lax.rem(face + 1, faces)
+    left, right = lax.rem(tile + tiles - 1, tiles), lax.rem(tile + 1, tiles)
+    halo = [(f, t) for f in (up, down) for t in (left, tile, right)]
+    halo += [(face, left), (face, right)]
+    for device in halo:
+        greet(device)
+    visit_near(greet)
+    visit_high(greet)
+    greeted = len(halo) + near_slots.shape[0] - 1 + high_slots.shape[0] - 1
 
     square = (LANES, LANES)
     ri, ci = iota(square, 0), iota(square, 1)
@@ -423,7 +419,7 @@
         both = jnp.concatenate([even, zero, odd, zero], axis=0)
         x0_ref[pl.ds(r, 2)] = both.T.reshape(2, ncols, LANES)
 
-    pl.semaphore_wait(barrier, devices - 1)
+    pl.semaphore_wait(barrier, greeted)
 
     def exchange(i, field, rows, fine, pack, unpack):
         cols = (fine_col_send, fine_col_recv) if fine else (coarse_col_send, coarse_col_recv)
@@ -537,8 +533,8 @@
         act, sig = soft(pre1[r * ncols : (r + 1) * ncols])
         act_sum = act_sum + act
         d1_ref[r] = sig
-    feature_sum = GroupSum(feature_slots, sum_sems.at[0], linear, to_everyone)
-    feature_sum.start(jnp.sum(act_sum, axis=0, keepdims=True))
+    feature_sums = group_sums(feature_near, feature_high, 3)
+    feature_sums[0].start(jnp.sum(act_sum, axis=0, keepdims=True))
 
     ex2 = exchange(2, d1_ref, (None, deep_rows_recv), False, None, None)
     ex2.start()
@@ -546,6 +542,7 @@
     row, lane = iota((nch0, LANES), 0), iota((nch0, LANES), 1)
     for r in range(nrows // 2):
         put(split_d1_ref, r, (0, 1), d1_ref[r])
+    feature_sums[1].start(feature_sums[0].finish())
     products = mm(split1_ref[...], split_d1_ref[...], 0, 0, None)
     unscaled = []
     for k in range(order):
@@ -553,7 +550,7 @@
         full = full + products[(order + k) * LANES : (order + k + 1) * LANES, :LANES]
         unscaled.append(jnp.sum((mask1 * full).reshape(-1, nch0, LANES), axis=0))
 
-    features = feature_sum.finish() / pooled
+    features = feature_sums[1].finish() / pooled
     hidden = jnp.tanh(mm3(split(head_mask * features), wf) + from_params)
     logits = jnp.sum(hidden * out_w_ref[...], axis=1, keepdims=True)
     logits_ref[...] = jnp.sum(jnp.where(spot, logits, 0.0), axis=0, keepdims=True)
@@ -604,21 +601,7 @@
         here = (row // nbins == k) & (lane // nch0 == order * nch1 // nch0)
         grads = jnp.where(here, part, grads)
 
-    low = tiles // high_slots.shape[0]
-    tile_high, tile_low = lax.div(tile, low), lax.rem(tile, low)
-    my_near = face * low + tile_low
-
-    def near_device(j):
-        return lax.div(j, low), tile_high * low + lax.rem(j, low)
-
-    groups = (
-        (near_slots, my_near, near_device),
-        (high_slots, tile_high, lambda j: (face, j * low + tile_low)),
-    )
-    sums = [
-        GroupSum(slots, sum_sems.at[1 + i], me, ring(me, slots.shape[0], device_of))
-        for i, (slots, me, device_of) in enumerate(groups)
-    ]
+    sums = group_sums(near_slots, high_slots, 1)
     sums[0].start(grads)
     def mix(x, first):
         return x + 2.0 * pltpu.roll(first, LANES - fields, axis=first.ndim - 1)
@@ -717,10 +700,11 @@
             buf(4, 4, 2, 1, LANES),
             pltpu.SemaphoreType.DMA((4, 8)),
             pltpu.SemaphoreType.DMA((4, 8)),
-            buf(faces * tiles, 1, LANES),
+            buf(faces * low, 1, LANES),
+            buf(tiles // low, 1, LANES),
             buf(faces * low, fine_w.shape[2], LANES),
             buf(tiles // low, fine_w.shape[2], LANES),
-            pltpu.SemaphoreType.DMA((4, 2)),
+            pltpu.SemaphoreType.DMA((5, 2)),
         ],
         compiler_params=pltpu.CompilerParams(
             collective_id=0, has_side_effects=True, vmem_limit_bytes=60 * 1024 * 1024

time: 35.2 us -> 36.3 us (1.031)
  Pallas kernels: 34.4 us -> 35.4 us
    pallas_call x1, Pallas kernels: 32.8 us -> 33.8 us  [on_device(): pl.pallas_call(functools.partial(kernel, faces, tiles), out_shape=tuple((...]
where the time goes in v6:
time: 36.3 us; the launch traced here: 36.1 us
  Pallas kernels  35.4 us (98%)
  between operations  0.64 us (2%)
    pallas_call x1, Pallas kernels, on_device(): pl.pallas_call(functools.partial(kernel, faces, tiles), out_shape=tuple((...  33.8 us
    pallas_call x1, Pallas kernels, on_device(): pl.pallas_call(write_kernel, out_shape=tuple((jax.ShapeDtypeStruct(x.shap...  1.64 us

profile of v6, /device:TPU:0, one launch (start us, length us, event | category | flops | bytes accessed | tf_op | source)
XLA Modules:
  0.0 36.1 jit_solution(13379550281515613959)
XLA Ops:
  0.6 33.8 %shard_map.120 = (f32[1,4]{1,0:T(1,128)}, f32[4,4,16,128]{3,2,1,0:T(8,128)}, f32[3,4,16]{2,1,0:T(4,128)}, f32[3,16,32]{2,1,0:T(8,128)}) custom-call(bf16[4,4,16,128]{3,2,1,0:T(8,128)(2,1)} %refs_0_.1, f32[2,4]{1,0:T(2,128)} %bitcast.4, s32[1,4]{1,0:T(1,128)} %bitcast.5, s32[2,16]{1,0:T(2,128)} %refs_3_.1, f32[3,4,16]{2,1,0:T(4,128)} %refs_4_.1, ...), custom_call_target="tpu_custom_call" | custom-call | tf_op jit(solution)/shard_map/pallas_call | solution.py:665
  34.4 1.6 %shard_map.121 = (f32[1,4]{1,0:T(1,128)}, f32[4,4,16,128]{3,2,1,0:T(8,128)}, f32[3,4,16]{2,1,0:T(4,128)}, f32[3,16,32]{2,1,0:T(8,128)}) custom-call(f32[1,4]{1,0:T(1,128)} %get-tuple-element.12.refs_0_, f32[4,4,16,128]{3,2,1,0:T(8,128)} %get-tuple-element.13.refs_1_, f32[3,4,16]{2,1,0:T(4,128)} %get-tuple-element.14.refs_2_, ...), custom_call_target="tpu_custom_call" | custom-call | tf_op jit(solution)/shard_map/pallas_call | solution.py:713
